TPU v7x, 32 devices: a whole 2x2x4 slice. The times are simulated.
32 devices in a mesh: dp: 8 (over z, y), mp: 4 (over x, core).
Axes of the slice: x: 2, y: 2, z: 4, core: 2. Of those that a mesh axis runs over, the one named last changes fastest.
Arguments:
- token_ids: int32 [128, 64], P(('dp', 'mp')), may hold values from 0 to 501152, as said below
- pair_index: int32 [64, 2], replicated, may hold values from 0 to 127, as said below
- table: bfloat16 [501248, 768], P(('dp', 'mp')), may hold values from -6 to 6
- query_key_value_weight: bfloat16 [768, 3, 768], P(None, None, 'mp'), may hold values from -0.21875 to 0.21875
- b_q: bfloat16 [768], P('mp'), may hold values from -3 to 3
- b_v: bfloat16 [768], P('mp'), may hold values from -3 to 3
- attention_output_weight: bfloat16 [768, 768], P('mp'), may hold values from -0.875 to 0.875
- b_o: bfloat16 [768], replicated, may hold values from -3 to 3
- ln1_gain: bfloat16 [768], replicated, may hold values from 0.25 to 1.75
- ln1_bias: bfloat16 [768], replicated, may hold values from -3 to 3
- feed_input_weight: bfloat16 [768, 3072], P(None, 'mp'), may hold values from -0.21875 to 0.21875
- feed_input_bias: bfloat16 [3072], P('mp'), may hold values from -3 to 3
- feed_output_weight: bfloat16 [3072, 768], P('mp'), may hold values from -0.15625 to 0.15625
- b_out: bfloat16 [768], replicated, may hold values from -3 to 3
- ln2_gain: bfloat16 [768], replicated, may hold values from 0.25 to 1.75
- ln2_bias: bfloat16 [768], replicated, may hold values from -3 to 3
- grad_out: float32 [128, 64, 768], P(('dp', 'mp')), may hold values from -6 to 6
Outputs:
- hidden: float32 [128, 64, 768], P(('dp', 'mp'))
- ranking_loss: float32 [], replicated
- table_grad: float32 [501248, 768], P(('dp', 'mp'))
- qkv_grad: float32 [768, 3, 768], P('dp', None, 'mp')
- q_bias_grad: float32 [768], P(('dp', 'mp'))
- v_bias_grad: float32 [768], P(('dp', 'mp'))
- o_grad: float32 [768, 768], P('mp', 'dp')
- o_bias_grad: float32 [768], P(('dp', 'mp'))
- ln1_gain_grad: float32 [768], P(('dp', 'mp'))
- ln1_bias_grad: float32 [768], P(('dp', 'mp'))
- in_grad: float32 [768, 3072], P('dp', 'mp')
- in_bias_grad: float32 [3072], P(('dp', 'mp'))
- out_grad: float32 [3072, 768], P('mp', 'dp')
- out_bias_grad: float32 [768], P(('dp', 'mp'))
- ln2_gain_grad: float32 [768], P(('dp', 'mp'))
- ln2_bias_grad: float32 [768], P(('dp', 'mp'))
Inputs may be any that keep to these rules, and one draw needn't show every extreme that they name: `token_ids`: ids name rows among the first 501153 of the 501248 table rows. Among the tokens of one device (an aligned block of 4 sentences), at most 16 ids lie in any one range of 15664 rows; one range holds exactly 16 ids of every device's block. `pair_index`: each of the 128 sentences appears exactly once.
All inputs are finite; a program needn't handle non-finite values.
Results may differ from a plain program's by a relative error of at most 0.018.
The roundings to bfloat16 on the way count: a program that leaves them out, or rounds other values in their place, can miss the bound.
Values may be sent and summed in bfloat16 or wider, within the bound.
No kernel may reach another device: no remote copies, remote signals or barrier semaphores. Data moves between devices by JAX's collectives and lax.ppermute only.
A program may use at most 192 MiB of HBM per device.

v0:
```python
import jax
import jax.numpy as jnp
from jax import lax
from jax.sharding import PartitionSpec as P

HEAD_DIM = 64


norm_eps = 1e-06
score_scale = 50.0
margin = 0.3
root_half = 0.7071067811865476
inv_root_tau = 0.3989422804014327
highest_value = lax.Precision.HIGHEST


def norm_forward(array_in, gain_vec, shift_vec):
    centre = array_in - jnp.mean(array_in, axis=-1, keepdims=True)
    inverse = lax.rsqrt(jnp.mean(centre * centre, axis=-1, keepdims=True) + norm_eps)
    normed = centre * inverse
    return (normed * gain_vec + shift_vec, normed, inverse)


def norm_backward(grad_in, normed, inverse, gain_vec):
    scaled = grad_in * gain_vec
    inner = (
        scaled
        - jnp.mean(scaled, axis=-1, keepdims=True)
        - normed * jnp.mean(scaled * normed, axis=-1, keepdims=True)
    )
    return (inner * inverse, jnp.sum(grad_in * normed, axis=0), jnp.sum(grad_in, axis=0))


def gelu_slope(array_in):
    return (
        0.5 * (1.0 + lax.erf(array_in * root_half))
        + array_in * jnp.exp(-0.5 * array_in * array_in) * inv_root_tau
    )


def split_heads(block_in, seq_len, head_dim):
    row_count, col_count = block_in.shape
    return block_in.reshape(row_count // seq_len, seq_len, col_count // head_dim, head_dim)


def attend(mixed_output, b_q, b_v, seq_len, head_dim):
    head_cols = b_q.shape[0]
    queries = split_heads(
        (mixed_output[:, :head_cols] + b_q).astype(jnp.bfloat16), seq_len, head_dim
    )
    key_rows = split_heads(
        mixed_output[:, head_cols : 2 * head_cols].astype(jnp.bfloat16), seq_len, head_dim
    )
    values = split_heads(
        (mixed_output[:, 2 * head_cols :] + b_v).astype(jnp.bfloat16), seq_len, head_dim
    )
    scores = jnp.einsum(
        "slhd,smhd->shlm", queries, key_rows, preferred_element_type=jnp.float32
    ) * head_dim ** (-0.5)
    row_peak = jnp.max(scores, axis=-1, keepdims=True)
    weights = jnp.exp(scores - row_peak)
    row_total = jnp.sum(weights, axis=-1, keepdims=True)
    log_total = row_peak + jnp.log(row_total)
    prob_low = (weights / row_total).astype(jnp.bfloat16)
    context_rows = jnp.einsum(
        "shlm,smhd->slhd", prob_low, values, preferred_element_type=jnp.float32
    )
    return (
        queries,
        key_rows,
        values,
        log_total,
        context_rows.astype(jnp.bfloat16).reshape(mixed_output.shape[0], head_cols),
    )


def attend_back(queries, key_rows, values, log_total, d_context, seq_len, head_dim):
    score_mult = head_dim ** (-0.5)
    scores = (
        jnp.einsum("slhd,smhd->shlm", queries, key_rows, preferred_element_type=jnp.float32)
        * score_mult
    )
    probs = jnp.exp(scores - log_total)
    d_ctx = split_heads(d_context, seq_len, head_dim)
    d_values = jnp.einsum(
        "shlm,slhd->smhd", probs.astype(jnp.bfloat16), d_ctx, preferred_element_type=jnp.float32
    ).astype(jnp.bfloat16)
    d_probs = jnp.einsum("slhd,smhd->shlm", d_ctx, values, preferred_element_type=jnp.float32)
    d_scores = (probs * (d_probs - jnp.sum(probs * d_probs, axis=-1, keepdims=True))).astype(
        jnp.bfloat16
    )
    d_queries = (
        jnp.einsum("shlm,smhd->slhd", d_scores, key_rows, preferred_element_type=jnp.float32)
        * score_mult
    ).astype(jnp.bfloat16)
    d_keys = (
        jnp.einsum("shlm,slhd->smhd", d_scores, queries, preferred_element_type=jnp.float32)
        * score_mult
    ).astype(jnp.bfloat16)
    row_count = d_context.shape[0]
    return jnp.concatenate(
        [
            d_queries.reshape(row_count, -1),
            d_keys.reshape(row_count, -1),
            d_values.reshape(row_count, -1),
        ],
        axis=1,
    )


def on_device(
    token_ids,
    pair_index,
    table,
    query_key_value_weight,
    b_q,
    b_v,
    attention_output_weight,
    b_o,
    ln1_gain,
    ln1_bias,
    feed_input_weight,
    feed_input_bias,
    feed_output_weight,
    b_out,
    ln2_gain,
    ln2_bias,
    grad_out,
):
    sent_loc, seq_len = token_ids.shape
    tok_loc = sent_loc * seq_len
    rows_shard, width = table.shape
    shards = lax.axis_size(("dp", "mp"))
    tensor = lax.axis_size("mp")
    capacity = 2 * tok_loc // shards
    head_cols = query_key_value_weight.shape[2]
    ffn_cols = feed_input_weight.shape[1]
    flat_qkv = query_key_value_weight.reshape(width, 3 * head_cols)
    flat_ids = token_ids.reshape(tok_loc)
    owners = flat_ids // rows_shard
    within_row = flat_ids - owners * rows_shard
    matches = (owners[:, None] == jnp.arange(shards, dtype=jnp.int32)[None, :]).astype(jnp.int32)
    slot_pos = jnp.sum(jnp.cumsum(matches, axis=0) * matches, axis=1) - 1
    requests = jnp.full((shards, capacity), -1, jnp.int32).at[owners, slot_pos].set(within_row)
    asked_rows = lax.all_to_all(requests, ("dp", "mp"), split_axis=0, concat_axis=0, tiled=True)
    picked_rows = jnp.take(table, jnp.maximum(asked_rows, 0), axis=0)
    fetched = lax.all_to_all(picked_rows, ("dp", "mp"), split_axis=0, concat_axis=0, tiled=True)
    x_rows = fetched[owners, slot_pos]

    def front(x_own):
        x_group = lax.all_gather(x_own, "mp", axis=0, tiled=True)
        mixed_output = jnp.dot(x_group, flat_qkv, preferred_element_type=jnp.float32)
        return (x_group,) + attend(mixed_output, b_q, b_v, seq_len, HEAD_DIM)

    x_group, queries, key_rows, values, log_total, context_rows = front(x_rows)
    attn_out = lax.psum_scatter(
        jnp.dot(context_rows, attention_output_weight, preferred_element_type=jnp.float32),
        "mp",
        scatter_dimension=0,
        tiled=True,
    )
    first_normed_rows, normed1, inverse1 = norm_forward(
        x_rows.astype(jnp.float32) + attn_out + b_o, ln1_gain, ln1_bias
    )
    first_low = first_normed_rows.astype(jnp.bfloat16)

    def ffn_front(h_own):
        h_group = lax.all_gather(h_own, "mp", axis=0, tiled=True)
        return (
            h_group,
            jnp.dot(h_group, feed_input_weight, preferred_element_type=jnp.float32)
            + feed_input_bias,
        )

    h_group, up_projected = ffn_front(first_low)
    gelu_activations = jax.nn.gelu(up_projected, approximate=False).astype(jnp.bfloat16)
    feed_forward_branch = lax.psum_scatter(
        jnp.dot(gelu_activations, feed_output_weight, preferred_element_type=jnp.float32),
        "mp",
        scatter_dimension=0,
        tiled=True,
    )
    hidden, normed2, inverse2 = norm_forward(
        first_normed_rows + feed_forward_branch + b_out, ln2_gain, ln2_bias
    )
    cls_rows = hidden.reshape(sent_loc, seq_len, width)[:, 0, :]
    radius = lax.rsqrt(jnp.sum(cls_rows * cls_rows, axis=-1, keepdims=True) + norm_eps)
    pooled = (cls_rows * radius).astype(jnp.bfloat16)
    all_pooled = lax.all_gather(pooled, ("dp", "mp"), axis=0, tiled=True)
    source = all_pooled[pair_index[:, 0]]
    target = all_pooled[pair_index[:, 1]]
    pair_count = pair_index.shape[0]
    eye_pairs = jnp.eye(pair_count, dtype=jnp.float32)
    logits = score_scale * (
        jnp.dot(source, target.T, preferred_element_type=jnp.float32) - margin * eye_pairs
    )
    row_peak = jnp.max(logits, axis=1, keepdims=True)
    row_exp = jnp.exp(logits - row_peak)
    row_sum = jnp.sum(row_exp, axis=1, keepdims=True)
    col_peak = jnp.max(logits, axis=0, keepdims=True)
    col_exp = jnp.exp(logits - col_peak)
    col_sum = jnp.sum(col_exp, axis=0, keepdims=True)
    row_lse = row_peak[:, 0] + jnp.log(row_sum[:, 0])
    col_lse = col_peak[0] + jnp.log(col_sum[0])
    loss_sum = 0.5 * jnp.sum(row_lse + col_lse) - jnp.sum(jnp.diagonal(logits))
    ranking_loss = loss_sum / pair_count
    d_logits = 0.5 * (row_exp / row_sum + col_exp / col_sum) - eye_pairs
    d_source = score_scale * jnp.dot(d_logits, target.astype(jnp.float32), precision=highest_value)
    d_target = score_scale * jnp.dot(
        d_logits.T, source.astype(jnp.float32), precision=highest_value
    )
    d_every = (
        jnp.zeros(all_pooled.shape, jnp.float32)
        .at[pair_index[:, 0]]
        .add(d_source)
        .at[pair_index[:, 1]]
        .add(d_target)
    )
    own_start = lax.axis_index(("dp", "mp")) * sent_loc
    d_pooled = lax.dynamic_slice_in_dim(d_every, own_start, sent_loc, 0)
    d_cls = radius * d_pooled - cls_rows * radius * radius * radius * jnp.sum(
        cls_rows * d_pooled, axis=-1, keepdims=True
    )
    d_hidden = grad_out.at[:, 0, :].add(d_cls).reshape(tok_loc, width)
    d_res2, d_gain2, d_shift2 = norm_backward(d_hidden, normed2, inverse2, ln2_gain)
    d_ffn = d_res2.astype(jnp.bfloat16)
    x_group, queries, key_rows, values, log_total, context_rows = front(x_rows)
    h_group, up_projected = ffn_front(first_low)
    activated_group = jax.nn.gelu(up_projected, approximate=False).astype(jnp.bfloat16)
    d_ffn_group = lax.all_gather(d_ffn, "mp", axis=0, tiled=True)
    d_act = jnp.einsum(
        "gd,fd->gf", d_ffn_group, feed_output_weight, preferred_element_type=jnp.float32
    )
    grad_w_out = jnp.einsum(
        "gf,gd->fd", activated_group, d_ffn_group, preferred_element_type=jnp.float32
    )
    d_up = (d_act * gelu_slope(up_projected)).astype(jnp.bfloat16)
    grad_b_in = jnp.sum(d_up.astype(jnp.float32), axis=0)
    grad_w_in = jnp.einsum("gd,gf->df", h_group, d_up, preferred_element_type=jnp.float32)
    d_first = d_res2 + lax.psum_scatter(
        jnp.einsum("gf,df->gd", d_up, feed_input_weight, preferred_element_type=jnp.float32),
        "mp",
        scatter_dimension=0,
        tiled=True,
    )
    d_res1, d_gain1, d_shift1 = norm_backward(d_first, normed1, inverse1, ln1_gain)
    d_att = d_res1.astype(jnp.bfloat16)
    d_att_group = lax.all_gather(d_att, "mp", axis=0, tiled=True)
    d_context = jnp.einsum(
        "gd,ed->ge", d_att_group, attention_output_weight, preferred_element_type=jnp.float32
    ).astype(jnp.bfloat16)
    grad_w_o = jnp.einsum(
        "ge,gd->ed", context_rows, d_att_group, preferred_element_type=jnp.float32
    )
    d_mixed = attend_back(queries, key_rows, values, log_total, d_context, seq_len, HEAD_DIM)
    grad_w_qkv = jnp.einsum(
        "gd,gc->dc", x_group, d_mixed, preferred_element_type=jnp.float32
    ).reshape(width, 3, head_cols)
    d_mixed_wide = d_mixed.astype(jnp.float32)
    grad_b_q = jnp.sum(d_mixed_wide[:, :head_cols], axis=0)
    grad_b_v = jnp.sum(d_mixed_wide[:, 2 * head_cols :], axis=0)
    d_emb = d_res1 + lax.psum_scatter(
        jnp.einsum("gc,dc->gd", d_mixed, flat_qkv, preferred_element_type=jnp.float32).astype(
            jnp.bfloat16
        ),
        "mp",
        scatter_dimension=0,
        tiled=True,
    ).astype(jnp.float32)
    qkv_part, o_part, in_part, out_part = (
        lax.psum_scatter(
            grad_w_qkv.astype(jnp.bfloat16), "dp", scatter_dimension=0, tiled=True
        ).astype(jnp.float32),
        lax.psum_scatter(
            grad_w_o.astype(jnp.bfloat16), "dp", scatter_dimension=1, tiled=True
        ).astype(jnp.float32),
        lax.psum_scatter(
            grad_w_in.astype(jnp.bfloat16), "dp", scatter_dimension=0, tiled=True
        ).astype(jnp.float32),
        lax.psum_scatter(
            grad_w_out.astype(jnp.bfloat16), "dp", scatter_dimension=1, tiled=True
        ).astype(jnp.float32),
    )
    share_cols = width // shards
    ffn_total = ffn_cols * tensor
    ffn_share = ffn_total // shards
    tensor_index = lax.axis_index("mp")
    shared = jnp.stack(
        [jnp.sum(d_res1, axis=0), d_gain1, d_shift1, jnp.sum(d_res2, axis=0), d_gain2, d_shift2]
    )
    head_biases = lax.dynamic_update_slice(
        jnp.zeros((2, width), jnp.float32),
        jnp.stack([grad_b_q, grad_b_v]),
        (0, tensor_index * head_cols),
    )
    ffn_bias = lax.dynamic_update_slice(
        jnp.zeros((ffn_total,), jnp.float32), grad_b_in, (tensor_index * ffn_cols,)
    )
    outgoing = jnp.concatenate(
        [
            shared.reshape(6, shards, share_cols)
            .transpose(1, 0, 2)
            .reshape(shards, 6 * share_cols),
            head_biases.reshape(2, shards, share_cols)
            .transpose(1, 0, 2)
            .reshape(shards, 2 * share_cols),
            ffn_bias.reshape(shards, ffn_share),
        ],
        axis=1,
    )
    sending = jnp.zeros((shards, capacity, width), jnp.float32).at[owners, slot_pos].set(d_emb)
    arrived, collected = (
        lax.all_to_all(
            sending.astype(jnp.bfloat16), ("dp", "mp"), split_axis=0, concat_axis=0, tiled=True
        ).astype(sending.dtype),
        lax.all_to_all(
            outgoing.astype(jnp.bfloat16), ("dp", "mp"), split_axis=0, concat_axis=0, tiled=True
        ).astype(outgoing.dtype),
    )
    live_mask = (asked_rows >= 0).astype(jnp.float32)[:, :, None]
    table_grad = (
        jnp.zeros((rows_shard, width), jnp.float32)
        .at[jnp.maximum(asked_rows, 0)]
        .add(arrived * live_mask)
    )
    totals = jnp.sum(collected, axis=0)
    shared_sum = totals[: 6 * share_cols].reshape(6, share_cols)
    heads_sum = totals[6 * share_cols : 8 * share_cols].reshape(2, share_cols)
    ffn_sum = totals[8 * share_cols :]
    return (
        hidden.reshape(sent_loc, seq_len, width),
        ranking_loss,
        table_grad,
        qkv_part,
        heads_sum[0],
        heads_sum[1],
        o_part,
        shared_sum[0],
        shared_sum[1],
        shared_sum[2],
        in_part,
        ffn_sum,
        out_part,
        shared_sum[3],
        shared_sum[4],
        shared_sum[5],
    )


def solution(mesh):
    in_specs = (
        P(("dp", "mp"), None),
        P(),
        P(("dp", "mp"), None),
        P(None, None, "mp"),
        P("mp"),
        P("mp"),
        P("mp", None),
        P(),
        P(),
        P(),
        P(None, "mp"),
        P("mp"),
        P("mp", None),
        P(),
        P(),
        P(),
        P(("dp", "mp"), None, None),
    )
    out_specs = (
        P(("dp", "mp"), None, None),
        P(),
        P(("dp", "mp"), None),
        P("dp", None, "mp"),
        P(("dp", "mp")),
        P(("dp", "mp")),
        P("mp", "dp"),
        P(("dp", "mp")),
        P(("dp", "mp")),
        P(("dp", "mp")),
        P("dp", "mp"),
        P(("dp", "mp")),
        P("mp", "dp"),
        P(("dp", "mp")),
        P(("dp", "mp")),
        P(("dp", "mp")),
    )
    return jax.shard_map(
        on_device, mesh=mesh, in_specs=in_specs, out_specs=out_specs, check_vma=False
    )
```

profile of v0, /device:TPU:0, one launch (start us, length us, event | category | flops | bytes accessed | tf_op | source)
XLA Modules:
  0.0 740.4 jit_solution(12569698598579415413)
XLA Ops:
  7.2 2.2 copy.233
  13.0 12.7 %scatter_fusion = s32[32,16]{0,1:T(8,128)S(1)} fusion(s32[32,16]{0,1:T(8,128)S(1)} %broadcast_in_dim.24, s32[256]{0:T(256)S(1)} %bitcast.138, s32[256]{0:T(256)S(1)} %get-tuple-element.51), kind=kCustom, calls=%fused_computation.5 | custom fusion | bytes 5120 | tf_op jit(solution)/shard_map/scatter | solution.py:144
  25.8 14.2 %all_to_all.25 = s32[32,1,16]{2,1,0:T(1,128)S(1)} all-to-all(s32[32,1,16]{2,1,0:T(1,128)S(1)} %copy.144), channel_id=1, replica_groups=mesh['dp'=8,'mp'=4] {'dp','mp'}, dimensions={0} | all-to-all | bytes 4096 | tf_op jit(solution)/shard_map/all_to_all | solution.py:145
  41.5 13.3 %gather_fusion = bf16[512,768]{1,0:T(8,128)(2,1)S(1)} fusion(bf16[15664,768]{1,0:T(8,128)(2,1)} %param.21, s32[1024]{0:T(1024)S(1)} %pad_clamp_fusion.2), kind=kCustom, calls=%fused_computation | custom fusion | bytes 1574912 | tf_op jit(solution)/shard_map/jit(_take)/gather | solution.py:146
  55.0 22.3 %all_to_all.26 = bf16[32,16,768]{2,1,0:T(8,128)(2,1)S(1)} all-to-all(bf16[32,16,768]{2,1,0:T(8,128)(2,1)S(1)} %broadcast_select_fusion), channel_id=1, replica_groups=mesh['dp'=8,'mp'=4] {'dp','mp'}, dimensions={0} | all-to-all | bytes 1572864 | tf_op jit(solution)/shard_map/all_to_all | solution.py:147
  77.4 3.2 gather_fusion.1
  81.2 18.1 %all-gather.6.cloned.1.call-done = bf16[1024,768]{1,0:T(8,128)(2,1)} async-done(((bf16[256,768]{1,0:T(8,128)(2,1)}), bf16[1024,768]{1,0:T(8,128)(2,1)}) %all-gather.6.cloned.1.call-update) | async-done | bytes 1572880 | tf_op jit(solution)/shard_map/all_gather | solution.py:151
  99.3 2.5 fusion.61
  102.6 1.4 reshape.441
  104.4 1.6 copy.157
  106.1 1.8 fusion.60
  108.9 1.4 copy.152
  110.3 1.8 reshape.442
  112.1 2.3 fusion.62
  115.1 37.4 %reduce-scatter.11.cloned.1.call-done = f32[256,768]{1,0:T(8,128)} async-done(((f32[1024,768]{1,0:T(8,128)}), f32[256,768]{1,0:T(8,128)}) %reduce-scatter.11.cloned.1.call-update) | async-done | bytes 786448 | tf_op jit(solution)/shard_map/reduce_scatter | solution.py:156
  152.5 1.4 fusion.57
  155.7 1.3 convert_element_type.192
  157.0 18.5 %all-gather.8.cloned.1.call-done = bf16[1024,768]{1,0:T(8,128)(2,1)} async-done(((bf16[256,768]{1,0:T(8,128)(2,1)}), bf16[1024,768]{1,0:T(8,128)(2,1)}) %all-gather.8.cloned.1.call-update) | async-done | bytes 1572880 | tf_op jit(solution)/shard_map/all_gather | solution.py:168
  175.5 10.1 %fusion.4 = (bf16[1024,768]{1,0:T(8,128)(2,1)S(1)}, f32[1024,768]{1,0:T(8,128)}) fusion(f32[768]{0:T(1024)} %convert_element_type.192, bf16[1024,768]{1,0:T(8,128)(2,1)} %all-gather.8.cloned.1.call-done, bf16[768,768]{1,0:T(8,128)(2,1)S(1)} %copy-done), kind=kOutput, calls=%fused_computation.16 | convolution fusion | flops 1259864064 | bytes 7474176 | tf_op jit(solution)/shard_map/dot_general | solution.py:171
  186.7 3.1 fusion.63
  190.7 1.3 convert_element_type.194
  192.0 1.3 convert_element_type.196
  193.3 1.5 slice.111
  196.6 31.3 %reduce-scatter.13.cloned.1.call-done = f32[256,768]{1,0:T(8,128)} async-done(((f32[1024,768]{1,0:T(8,128)}), f32[256,768]{1,0:T(8,128)}) %reduce-scatter.13.cloned.1.call-update) | async-done | bytes 786448 | tf_op jit(solution)/shard_map/reduce_scatter | solution.py:177
  227.9 1.5 fusion.56
  232.2 43.7 %all-gather = bf16[32,4,768]{2,1,0:T(4,128)(2,1)} all-gather(bf16[1,4,768]{2,1,0:T(4,128)(2,1)S(1)} %fusion.47), channel_id=1, replica_groups=mesh['dp'=8,'mp'=4] {'dp','mp'}, dimensions={0}, use_global_device_ids=true | all-gather | bytes 202752 | tf_op jit(solution)/shard_map/all_gather | solution.py:189
  275.9 1.7 reshape.529
  277.6 2.5 gather_fusion.3
  280.1 2.5 gather_fusion.2
  284.0 2.0 convolution_multiply_fusion.1
  286.0 1.9 convolution_multiply_fusion.2
  287.9 2.1 scatter_custom_fusion.1
  290.0 3.1 scatter_fusion.1
  295.4 1.6 scatter-add.28
  296.9 1.7 fusion.28
  298.6 1.3 fusion.52
  301.1 1.3 div.98
  302.4 2.3 fusion.54
  306.5 15.9 %all-gather.10.cloned.1.call-done = bf16[1024,768]{1,0:T(8,128)(2,1)} async-done(((bf16[256,768]{1,0:T(8,128)(2,1)}), bf16[1024,768]{1,0:T(8,128)(2,1)}) %all-gather.10.cloned.1.call-update) | async-done | bytes 1572880 | tf_op jit(solution)/shard_map/all_gather | solution.py:230
  322.4 5.4 convert_reduce_fusion
  328.9 3.1 fusion.64
  332.1 38.1 %reduce-scatter.15.cloned.1.call-done = f32[256,768]{1,0:T(8,128)} async-done(((f32[1024,768]{1,0:T(8,128)}), f32[256,768]{1,0:T(8,128)}) %reduce-scatter.15.cloned.1.call-update) | async-done | bytes 786448 | tf_op jit(solution)/shard_map/reduce_scatter | solution.py:240
  370.2 2.2 multiply_reduce_fusion.1
  374.4 19.5 %all-gather.12.cloned.1.call-done = bf16[1024,768]{1,0:T(8,128)(2,1)} async-done(((bf16[256,768]{1,0:T(8,128)(2,1)}), bf16[1024,768]{1,0:T(8,128)(2,1)}) %all-gather.12.cloned.1.call-update) | async-done | bytes 1572880 | tf_op jit(solution)/shard_map/all_gather | solution.py:248
  394.0 2.8 convolution_convert_fusion.6
  396.8 1.7 reshape.446
  405.6 4.2 convolution_convert_fusion
  409.8 4.4 convolution_convert_fusion.1
  414.4 4.1 convolution_convert_fusion.2
  420.0 1.5 convert_element_type.220
  421.6 1.9 convolution_convert_fusion.7
  424.5 3.8 convolution_convert_fusion.3
  428.3 2.4 copy.171
  433.2 4.5 all-to-all-start.3
  439.6 13.9 %scatter_fusion.2 = f32[32,16,768]{2,1,0:T(8,128)S(1)} fusion(f32[32,16,768]{2,1,0:T(8,128)S(1)} %broadcast_in_dim.28, s32[256]{0:T(256)S(1)} %bitcast.139, f32[256,768]{1,0:T(8,128)S(1)} %convert_add_fusion), kind=kCustom, calls=%fused_computation.8 | custom fusion | bytes 2361344 | tf_op jit(solution)/shard_map/scatter | solution.py:311
  454.6 5.8 all-to-all-start.2
  463.8 46.1 %reduce-scatter.23.cloned.1.call-done = bf16[768,96]{0,1:T(8,128)(2,1)} async-done(((bf16[768,768]{0,1:T(8,128)(2,1)}), bf16[768,96]{0,1:T(8,128)(2,1)}) %reduce-scatter.23.cloned.1.call-update) | async-done | bytes 147472 | tf_op jit(solution)/shard_map/reduce_scatter | solution.py:280
  509.9 1.6 convert_element_type.228
  511.5 64.8 %reduce-scatter.21.cloned.1.call-done = bf16[96,768]{1,0:T(8,128)(2,1)} async-done(((bf16[768,768]{1,0:T(8,128)(2,1)}), bf16[96,768]{1,0:T(8,128)(2,1)}) %reduce-scatter.21.cloned.1.call-update) | async-done | bytes 147472 | tf_op jit(solution)/shard_map/reduce_scatter | solution.py:277
  576.3 1.6 convert_element_type.226
  579.4 60.6 %reduce-scatter.25.cloned.1.call-done = bf16[96,192]{1,0:T(8,128)(2,1)} async-done(((bf16[768,192]{1,0:T(8,128)(2,1)}), bf16[96,192]{1,0:T(8,128)(2,1)}) %reduce-scatter.25.cloned.1.call-update) | async-done | bytes 36880
  641.5 64.7 %reduce-scatter.19.cloned.1.call-done = bf16[96,3,192]{2,0,1:T(8,128)(2,1)} async-done(((bf16[768,3,192]{2,0,1:T(8,128)(2,1)}), bf16[96,3,192]{2,0,1:T(8,128)(2,1)}) %reduce-scatter.19.cloned.1.call-update) | async-done | bytes 110608 | tf_op jit(solution)/shard_map/reduce_scatter | solution.py:271
  706.2 1.6 convert_element_type.219
  708.1 23.8 %scatter_custom_fusion.4 = f32[15664,768]{1,0:T(8,128)} fusion(s32[512]{0:T(512)} %copy-done.38, f32[512,768]{1,0:T(8,128)S(1)} %bitcast.142, f32[]{:T(128)} %constant.68.clone.1), kind=kCustom, calls=%fused_computation.10 | custom fusion | flops 393216 | bytes 48120320 | tf_op jit(solution)/shard_map/scatter-add | solution.py:324
  (277 shorter events, 47.1 us)
Async XLA Ops:
  7.2 168.3 %copy-start = (bf16[768,768]{1,0:T(8,128)(2,1)S(1)}, bf16[768,768]{1,0:T(8,128)(2,1)}, u32[]{:S(2)}) copy-start(bf16[768,768]{1,0:T(8,128)(2,1)} %param.29) | copy-start | bytes 3538948
  7.2 92.1 %all-gather.6.cloned.1.call-start = ((), (), s32[]{:S(2)}) async-start(), calls=%async_computation.12 | async-start | bytes 1966080 | tf_op jit(solution)/shard_map/all_gather | solution.py:151
  77.4 3.8 copy-start.59
  77.4 3.8 copy-start.60
  77.4 21.9 %copy-start.58 = (bf16[768,3,192]{0,2,1:T(8,128)(2,1)S(1)}, bf16[768,3,192]{0,2,1:T(8,128)(2,1)}, u32[]{:S(2)}) copy-start(bf16[768,3,192]{0,2,1:T(8,128)(2,1)} %param.22) | copy-start | bytes 2654212
  80.6 71.9 %reduce-scatter.11.cloned.1.call-start = ((), (), s32[]{:S(2)}) async-start(), calls=%async_computation.13 | async-start | bytes 3932160 | tf_op jit(solution)/shard_map/reduce_scatter | solution.py:156
  102.5 5.3 copy-start.5
  106.1 2.2 copy-start.14
  108.9 3.2 copy-start.20
  112.1 2.3 copy-start.12
  114.4 61.1 %all-gather.8.cloned.1.call-start = ((), (), s32[]{:S(2)}) async-start(), calls=%async_computation.14 | async-start | bytes 1966080 | tf_op jit(solution)/shard_map/all_gather | solution.py:168
  115.1 112.8 %copy-start.24 = (f32[768]{0:T(1024)}, f32[768]{0:T(1024)S(1)}, u32[]{:S(2)}) copy-start(f32[768]{0:T(1024)S(1)} %convert_element_type.189) | copy-start | bytes 9220
  115.1 70.5 %copy-start.30 = (f32[768]{0:T(1024)}, f32[768]{0:T(1024)S(1)}, u32[]{:S(2)}) copy-start(f32[768]{0:T(1024)S(1)} %convert_element_type.190) | copy-start | bytes 9220
  153.9 74.0 %copy-start.28 = (f32[256]{0:T(256)}, f32[256]{0:T(256)S(1)}, u32[]{:S(2)}) copy-start(f32[256]{0:T(256)S(1)} %broadcast_multiply_fusion.5) | copy-start | bytes 3076
  155.7 72.2 %reduce-scatter.13.cloned.1.call-start = ((), (), s32[]{:S(2)}) async-start(), calls=%async_computation.15 | async-start | bytes 3932160 | tf_op jit(solution)/shard_map/reduce_scatter | solution.py:177
  175.5 11.2 %copy-start.57 = (bf16[768,768]{1,0:T(8,128)(2,1)S(1)}, bf16[768,768]{1,0:T(8,128)(2,1)}, u32[]{:S(2)}) copy-start(bf16[768,768]{1,0:T(8,128)(2,1)} %param.31) | copy-start | bytes 3538948
  185.6 1.1 copy-start.61
  189.8 132.6 %all-gather.10.cloned.1.call-start = ((), (), s32[]{:S(2)}) async-start(), calls=%async_computation.16 | async-start | bytes 1966080 | tf_op jit(solution)/shard_map/all_gather | solution.py:230
  190.7 39.9 %copy-start.26 = (f32[768]{0:T(1024)}, f32[768]{0:T(1024)S(1)}, u32[]{:S(2)}) copy-start(f32[768]{0:T(1024)S(1)} %convert_element_type.195) | copy-start | bytes 9220
  227.9 2.5 copy-start.35
  229.4 1.2 copy-start.34
  230.4 1.2 copy-start.36
  283.8 2.2 copy-start.3
  283.8 2.2 copy-start.41
  283.8 2.2 copy-start.43
  284.0 2.0 copy-start.46
  284.0 2.0 copy-start.48
  294.7 7.7 %copy-start.27 = (f32[768]{0:T(1024)S(1)}, f32[768]{0:T(1024)}, u32[]{:S(2)}) copy-start(f32[768]{0:T(1024)} %copy-done.26) | copy-start | bytes 9220
  306.4 63.7 %reduce-scatter.15.cloned.1.call-start = ((), (), s32[]{:S(2)}) async-start(), calls=%async_computation.17 | async-start | bytes 3932160 | tf_op jit(solution)/shard_map/reduce_scatter | solution.py:240
  327.8 1.2 copy-start.62
  332.0 38.2 %copy-start.11 = (f32[256,768]{1,0:T(8,128)S(1)}, f32[256,768]{1,0:T(8,128)}, u32[]{:S(2)}) copy-start(f32[256,768]{1,0:T(8,128)} %copy-done.10) | copy-start | bytes 2359300
  332.0 38.2 %copy-start.25 = (f32[768]{0:T(1024)S(1)}, f32[768]{0:T(1024)}, u32[]{:S(2)}) copy-start(f32[768]{0:T(1024)} %copy-done.24) | copy-start | bytes 9220
  332.0 38.2 %copy-start.29 = (f32[256]{0:T(256)S(1)}, f32[256]{0:T(256)}, u32[]{:S(2)}) copy-start(f32[256]{0:T(256)} %copy-done.28) | copy-start | bytes 3076
  332.1 38.2 %copy-start.33 = (f32[256]{0:T(256)S(1)}, f32[256]{0:T(256)}, u32[]{:S(2)}) copy-start(f32[256]{0:T(256)} %copy-done.32) | copy-start | bytes 3076
  332.1 61.9 %all-gather.12.cloned.1.call-start = ((), (), s32[]{:S(2)}) async-start(), calls=%async_computation.18 | async-start | bytes 1966080 | tf_op jit(solution)/shard_map/all_gather | solution.py:248
  372.4 2.0 copy-start.19
  372.4 2.0 copy-start.23
  372.4 21.6 %copy-start.21 = (bf16[192,768]{1,0:T(8,128)(2,1)S(1)}, bf16[192,768]{1,0:T(8,128)(2,1)}, u32[]{:S(2)}) copy-start(bf16[192,768]{1,0:T(8,128)(2,1)} %param.25) | copy-start | bytes 884740
  373.3 20.7 %copy-start.8 = (f32[256,768]{1,0:T(8,128)}, f32[256,768]{1,0:T(8,128)S(1)}, u32[]{:S(2)}) copy-start(f32[256,768]{1,0:T(8,128)S(1)} %get-tuple-element.45) | copy-start | bytes 2359300
  374.1 64.2 %reduce-scatter.17.cloned.1.call-start = ((), (), s32[]{:S(2)}) async-start(), calls=%async_computation.19 | async-start | bytes 1966080 | tf_op jit(solution)/shard_map/reduce_scatter | solution.py:262
  396.8 2.3 copy-start.15
  399.7 1.1 copy-start.6
  399.7 1.7 copy-start.7
  405.5 4.2 copy-start.16
  409.8 4.6 copy-start.56
  409.8 100.1 %reduce-scatter.23.cloned.1.call-start = ((), (), s32[]{:S(2)}) async-start(), calls=%async_computation.22 | async-start | bytes 1327104 | tf_op jit(solution)/shard_map/reduce_scatter | solution.py:280
  414.3 4.5 copy-start.39
  414.3 4.8 copy-start.54
  414.3 5.3 copy-start.40
  414.3 5.4 copy-start.37
  414.3 162.0 %reduce-scatter.21.cloned.1.call-start = ((), (), s32[]{:S(2)}) async-start(), calls=%async_computation.21 | async-start | bytes 1327104 | tf_op jit(solution)/shard_map/reduce_scatter | solution.py:277
  418.5 3.1 copy-start.13
  418.5 221.5 %reduce-scatter.25.cloned.1.call-start = ((), (), s32[]{:S(2)}) async-start(), calls=%async_computation.23 | async-start | bytes 442368
  428.3 10.1 %copy-start.9 = (f32[256,768]{1,0:T(8,128)S(1)}, f32[256,768]{1,0:T(8,128)}, u32[]{:S(2)}) copy-start(f32[256,768]{1,0:T(8,128)} %copy-done.8) | copy-start | bytes 2359300
  433.2 21.3 %all-to-all-start.3 = ((bf16[32,2,144]{2,1,0:T(2,128)(2,1)}), bf16[32,2,144]{2,1,0:T(2,128)(2,1)S(1)}, u32[]{:S(2)}, u32[]{:S(2)}) async-start(bf16[32,2,144]{2,1,0:T(2,128)(2,1)} %reshape.537), calls=%async_computation.8 | async-start | bytes 65536 | tf_op jit(solution)/shard_map/all_to_all | solution.py:316
  437.8 268.5 %reduce-scatter.19.cloned.1.call-start = ((), (), s32[]{:S(2)}) async-start(), calls=%async_computation.20 | async-start | bytes 1327104 | tf_op jit(solution)/shard_map/reduce_scatter | solution.py:271
  453.5 6.9 copy-start.31
  453.5 7.0 copy-start.4
  453.5 8.4 %copy-start.42 = (f32[64]{0:T(128)S(1)}, f32[64]{0:T(128)}, u32[]{:S(2)}) copy-start(f32[64]{0:T(128)} %copy-done.41) | copy-start | bytes 772
  453.6 8.4 %copy-start.44 = (f32[64]{0:T(128)S(1)}, f32[64]{0:T(128)}, u32[]{:S(2)}) copy-start(f32[64]{0:T(128)} %copy-done.43) | copy-start | bytes 772
  453.6 8.4 %copy-start.47 = (f32[64]{0:T(128)S(1)}, f32[64]{0:T(128)}, u32[]{:S(2)}) copy-start(f32[64]{0:T(128)} %copy-done.46) | copy-start | bytes 772
  453.6 8.4 %copy-start.49 = (f32[64]{0:T(128)S(1)}, f32[64]{0:T(128)}, u32[]{:S(2)}) copy-start(f32[64]{0:T(128)} %copy-done.48) | copy-start | bytes 772
  454.6 253.3 %all-to-all-start.2 = ((bf16[32,16,768]{2,1,0:T(8,128)(2,1)}), bf16[32,16,768]{2,1,0:T(8,128)(2,1)S(1)}, u32[]{:S(2)}, u32[]{:S(2)}) async-start(bf16[32,16,768]{2,1,0:T(8,128)(2,1)} %convert_element_type.213), calls=%async_computation.6 | async-start | bytes 1572864 | tf_op jit(solution)/shard_map/all_to_all | solution.py:313
  708.1 23.8 %copy-start.1 = (bf16[768,768]{1,0:T(8,128)(2,1)S(1)}, bf16[768,768]{1,0:T(8,128)(2,1)}, u32[]{:S(2)}) copy-start(bf16[768,768]{1,0:T(8,128)(2,1)} %param.29) | copy-start | bytes 3538948
  (13 other events, 9.1 us)
Sparse Core Ops, SparseCore 0:
  80.7 18.5 all-gather.5
  114.5 37.9 reduce-scatter.10
  155.8 19.6 all-gather.7
  189.9 37.9 reduce-scatter.12
  306.6 15.7 all-gather.9
  332.2 37.9 reduce-scatter.14
  374.3 19.6 all-gather.11
  409.9 28.1 reduce-scatter.16
  441.5 68.3 reduce-scatter.22
  513.1 63.1 reduce-scatter.20
  579.6 60.3 reduce-scatter.24
  643.2 62.9 reduce-scatter.18
where the time goes:
time: 748 us; the launch traced here: 740 us
  waiting for transfers between devices  416 us (56%)
  local copies, waits for them, and re-layouts  88.9 us (12%)
  blocking collectives  80.3 us (11%)
  other arithmetic  68 us (9%)
  matrix products  57.3 us (8%)
  between operations  18.2 us (2%)
  starting transfers between devices  12 us (2%)
    reduce_scatter x1, waiting for transfers between devices, on_device(): lax.psum_scatter(grad_w_in.astype(jnp.bfloat16), 'dp', scatter_dimension=...  64.8 us
    reduce_scatter x1, waiting for transfers between devices, on_device(): lax.psum_scatter(grad_w_qkv.astype(jnp.bfloat16), 'dp', scatter_dimension...  64.7 us
    unnamed x13, waiting for transfers between devices  61.3 us
    reduce_scatter x1, waiting for transfers between devices, on_device(): lax.psum_scatter(grad_w_out.astype(jnp.bfloat16), 'dp', scatter_dimension...  46.1 us
    all_gather x1, blocking collectives, on_device(): all_pooled = lax.all_gather(pooled, ('dp', 'mp'), axis=0, tiled=True)  43.7 us
    reduce_scatter x1, waiting for transfers between devices, on_device(): lax.psum_scatter(jnp.einsum('gf,df->gd', d_up, feed_input_weight, preferr...  38.1 us
    reduce_scatter x1, waiting for transfers between devices, on_device(): lax.psum_scatter(jnp.dot(context_rows, attention_output_weight, preferred...  37.4 us
    reduce_scatter x1, waiting for transfers between devices, on_device(): lax.psum_scatter(jnp.dot(gelu_activations, feed_output_weight, preferred_...  31.3 us
  transfers between devices with their start and end apart: 14, of which 11 were waited for; matrix products, arithmetic and copies ran while one was open for 8% of the time, Pallas kernels for 0%

commit v1 on v0

v1 whole, which is shorter than its diff:
```python
import functools

import jax
import jax.numpy as jnp
from jax import lax
from jax.experimental import pallas as pl
from jax.experimental.pallas import tpu as pltpu
from jax.sharding import PartitionSpec as P

HEAD_DIM = 64

norm_eps = 1e-06
score_scale = 50.0
margin = 0.3
root_half = 0.7071067811865476
inv_root_tau = 0.3989422804014327
highest_value = lax.Precision.HIGHEST
masked_out = -1e30

bf16 = jnp.bfloat16
f32 = jnp.float32
VMEM_LIMIT = 60 * 1024 * 1024


def dot(a, b):
    return jnp.dot(a, b, preferred_element_type=f32)


def dot_nt(a, b):
    return lax.dot_general(a, b, (((1,), (1,)), ((), ())), preferred_element_type=f32)


def dot_tn(a, b):
    return lax.dot_general(a, b, (((0,), (0,)), ((), ())), preferred_element_type=f32)


def mean_rows(v):
    return jnp.mean(v, axis=-1, keepdims=True)


def head_mask(rows, cols, head):
    lane = lax.broadcasted_iota(jnp.int32, (rows, cols), 1)
    return ((lane >= head * HEAD_DIM) & (lane < (head + 1) * HEAD_DIM)).astype(bf16)


def front_kernel(
    seq, fetched, pos, a0, a1, a2, a3, vec, x_out, qkv_out, prob_out, ctx_out, norm_out, inv_out,
    bias_out,
):
    tok, width = x_out.shape
    slots = fetched.shape[0]
    hc = ctx_out.shape[2]
    heads = hc // HEAD_DIM
    span = 2 * seq
    spans = tok // span
    hot = (lax.broadcasted_iota(jnp.int32, (tok, slots), 1) == pos[...]).astype(bf16)
    x32 = dot(hot, fetched[...])
    x = x32.astype(bf16)
    x_out[...] = x
    row_sent = lax.broadcasted_iota(jnp.int32, (span, span), 0) // seq
    col_sent = lax.broadcasted_iota(jnp.int32, (span, span), 1) // seq
    same = row_sent == col_sent
    res = x32 + vec[0:1, :]
    for r, a in enumerate((a0, a1, a2, a3)):
        bias = a[width : width + 16, :].astype(f32)
        bias_out[r : r + 1, :] = bias[1:2, :]
        mixed = dot(x, a[0:width, 0 : 3 * hc])
        q = (mixed[:, 0:hc] + bias[0:1, 0:hc]).astype(bf16)
        k = mixed[:, hc : 2 * hc].astype(bf16)
        v = (mixed[:, 2 * hc : 3 * hc] + bias[0:1, hc : 2 * hc]).astype(bf16)
        qkv_out[r, 0] = q
        qkv_out[r, 1] = k
        qkv_out[r, 2] = v
        for p in range(spans):
            rows = slice(p * span, (p + 1) * span)
            ctx = jnp.zeros((span, hc), f32)
            for h in range(heads):
                mask = head_mask(span, hc, h)
                s = dot_nt(q[rows] * mask, k[rows]) * HEAD_DIM ** (-0.5)
                s = jnp.where(same, s, masked_out)
                e = jnp.exp(s - jnp.max(s, axis=1, keepdims=True))
                prob = e / jnp.sum(e, axis=1, keepdims=True)
                prob_out[(r * spans + p) * heads + h] = prob
                ctx = ctx + dot(prob.astype(bf16), v[rows] * mask)
            ctx_out[r, rows, :] = ctx.astype(bf16)
        res = res + dot_nt(ctx_out[r], a[0:width, 3 * hc : 3 * hc + hc])
    centre = res - mean_rows(res)
    inverse = lax.rsqrt(mean_rows(centre * centre) + norm_eps)
    norm_out[...] = centre * inverse
    inv_out[...] = inverse


def ffn_kernel(
    seq, norm1, vec, f0, f1, f2, f3, biases,
    h_out, act_out, slope_out, hid_out, norm_out, inv_out, cls_out, pool_out, first, h, up, acc,
):
    tok, width = norm1.shape
    cols = act_out.shape[2]
    step = 32
    g1, s1 = vec[1:2, :], vec[2:3, :]

    def chunk(i):
        return pl.ds(pl.multiple_of(i * step, step), step)

    @pl.loop(0, tok // step)
    def _(i):
        v = norm1[chunk(i), :] * g1 + s1
        first[chunk(i), :] = v
        h[chunk(i), :] = v.astype(bf16)

    h_out[...] = h[...]
    for r, f in enumerate((f0, f1, f2, f3)):
        bias = biases[r : r + 1, :]
        up[...] = dot(h[...], f[0:width, :])

        @pl.loop(0, tok // step)
        def _(i, r=r, bias=bias):
            u = up[chunk(i), :] + bias
            cdf = 0.5 * (1.0 + lax.erf(u * root_half))
            act_out[r, chunk(i), :] = (u * cdf).astype(bf16)
            slope_out[r, chunk(i), :] = cdf + u * jnp.exp(-0.5 * u * u) * inv_root_tau

        part = dot(act_out[r], f[width:, :])
        if r == 0:
            acc[...] = part
        else:
            acc[...] += part
    bo, g2, s2 = vec[3:4, :], vec[4:5, :], vec[5:6, :]

    @pl.loop(0, tok // step)
    def _(i):
        res = first[chunk(i), :] + acc[chunk(i), :] + bo
        centre = res - mean_rows(res)
        inverse = lax.rsqrt(mean_rows(centre * centre) + norm_eps)
        normed = centre * inverse
        norm_out[chunk(i), :] = normed
        inv_out[chunk(i), :] = inverse
        hid_out[chunk(i), :] = normed * g2 + s2

    sent = pool_out.shape[0]
    for s in range(sent):
        cls_out[s : s + 1, :] = hid_out[s * seq : s * seq + 1, :]
    c = cls_out[...]
    radius = lax.rsqrt(jnp.sum(c * c, axis=-1, keepdims=True) + norm_eps)
    pool_out[...] = (c * radius).astype(bf16)


def back_ffn_kernel(
    seq, pooled, pair, pair_own, cls, grad_out, norm2, inv2, vec, h, act, slope, f0, f1, f2, f3,
    loss_out, dfirst_out, keep_out, send_out, sum_out, dh, dffn, dup, dact,
):
    tok, width = grad_out.shape
    cols = act.shape[2]
    pairs = pair.shape[0]
    sents = pooled.shape[0]
    sent = cls.shape[0]
    step = 32
    every = pooled[...]
    lane = lax.broadcasted_iota(jnp.int32, (pairs, sents), 1)
    source = dot((lane == pair[:, 0:1]).astype(bf16), every)
    target = dot((lane == pair[:, 1:2]).astype(bf16), every)
    at_row = lax.broadcasted_iota(jnp.int32, (pairs, pairs), 0)
    at_col = lax.broadcasted_iota(jnp.int32, (pairs, pairs), 1)
    eye = (at_row == at_col).astype(f32)
    logits = score_scale * (dot_nt(source.astype(bf16), target.astype(bf16)) - margin * eye)
    row_peak = jnp.max(logits, axis=1, keepdims=True)
    row_exp = jnp.exp(logits - row_peak)
    row_sum = jnp.sum(row_exp, axis=1, keepdims=True)
    col_peak = jnp.max(logits, axis=0, keepdims=True)
    col_exp = jnp.exp(logits - col_peak)
    col_sum = jnp.sum(col_exp, axis=0, keepdims=True)
    total = (
        0.5 * jnp.sum(row_peak + jnp.log(row_sum), axis=0, keepdims=True)
        + 0.5 * jnp.sum(col_peak + jnp.log(col_sum), axis=1, keepdims=True)
        - jnp.sum(jnp.sum(logits * eye, axis=1, keepdims=True), axis=0, keepdims=True)
    )
    loss_out[...] = total / pairs
    d_logits = 0.5 * (row_exp / row_sum + col_exp / col_sum) - eye
    own = lax.broadcasted_iota(jnp.int32, (8, pairs), 0)
    own_source = (own == pair_own[0:1, :]).astype(f32)
    own_target = (own == pair_own[1:2, :]).astype(f32)
    from_source = jnp.dot(own_source, d_logits, precision=highest_value, preferred_element_type=f32)
    from_target = lax.dot_general(
        own_target, d_logits, (((1,), (1,)), ((), ())), precision=highest_value,
        preferred_element_type=f32,
    )
    d_pooled = score_scale * (
        jnp.dot(from_source, target, precision=highest_value, preferred_element_type=f32)
        + jnp.dot(from_target, source, precision=highest_value, preferred_element_type=f32)
    )[0:sent]
    c = cls[...]
    radius = lax.rsqrt(jnp.sum(c * c, axis=-1, keepdims=True) + norm_eps)
    d_cls = radius * d_pooled - c * radius * radius * radius * jnp.sum(
        c * d_pooled, axis=-1, keepdims=True
    )
    dh[...] = grad_out[...]
    for s in range(sent):
        dh[s * seq : s * seq + 1, :] += d_cls[s : s + 1, :]
    g2 = vec[4:5, :]

    def chunk(i):
        return pl.ds(pl.multiple_of(i * step, step), step)

    zero = jnp.zeros((1, width), f32)

    def norm_back(i, sums):
        grad = dh[chunk(i), :]
        normed = norm2[chunk(i), :]
        e = grad * g2
        d_res = (e - mean_rows(e) - normed * mean_rows(e * normed)) * inv2[chunk(i), :]
        dfirst_out[chunk(i), :] = d_res
        dffn[chunk(i), :] = d_res.astype(bf16)
        return (
            sums[0] + jnp.sum(d_res, axis=0, keepdims=True),
            sums[1] + jnp.sum(grad * normed, axis=0, keepdims=True),
            sums[2] + jnp.sum(grad, axis=0, keepdims=True),
        )

    sums = lax.fori_loop(0, tok // step, norm_back, (zero, zero, zero))
    for i in range(3):
        sum_out[i : i + 1, :] = sums[i]
    sum_out[7:8, :] = zero
    d_ffn_t = dffn[...].T
    h_t = h[...].T
    for r, f in enumerate((f0, f1, f2, f3)):
        dact[...] = dot_nt(dffn[...], f[width:, :])

        def through(i, total, r=r):
            d_up = (dact[chunk(i), :] * slope[r, chunk(i), :]).astype(bf16)
            dup[chunk(i), :] = d_up
            return total + jnp.sum(d_up.astype(f32), axis=0, keepdims=True)

        sum_out[3 + r : 4 + r, :] = lax.fori_loop(
            0, tok // step, through, jnp.zeros((1, cols), f32)
        )
        dfirst_out[...] += dot_nt(dup[...], f[0:width, :])
        out = send_out if r % 2 else keep_out
        out[r // 2, 0] = dot(h_t, dup[...]).astype(bf16)
        out[r // 2, 1] = dot(d_ffn_t, act[r]).astype(bf16)


def back_attend_kernel(
    seq, dfirst, norm1, inv1, vec, x, qkv, prob, ctx, pos, a0, a1, a2, a3,
    keep_out, send_out, slot_out, sum_out, head_out, datt, dres,
):
    tok, width = dfirst.shape
    hc = ctx.shape[2]
    heads = hc // HEAD_DIM
    span = 2 * seq
    spans = tok // span
    step = 32
    g1 = vec[1:2, :]

    def chunk(i):
        return pl.ds(pl.multiple_of(i * step, step), step)

    zero = jnp.zeros((1, width), f32)

    def norm_back(i, sums):
        grad = dfirst[chunk(i), :]
        normed = norm1[chunk(i), :]
        e = grad * g1
        d_res = (e - mean_rows(e) - normed * mean_rows(e * normed)) * inv1[chunk(i), :]
        dres[chunk(i), :] = d_res
        datt[chunk(i), :] = d_res.astype(bf16)
        return (
            sums[0] + jnp.sum(d_res, axis=0, keepdims=True),
            sums[1] + jnp.sum(grad * normed, axis=0, keepdims=True),
            sums[2] + jnp.sum(grad, axis=0, keepdims=True),
        )

    sums = lax.fori_loop(0, tok // step, norm_back, (zero, zero, zero))
    for i in range(3):
        sum_out[i : i + 1, :] = sums[i]
    sum_out[3:8, :] = jnp.zeros((5, width), f32)
    d_att_t = datt[...].T
    x_t = x[...].T
    for r, a in enumerate((a0, a1, a2, a3)):
        d_ctx = dot(datt[...], a[0:width, 3 * hc : 4 * hc]).astype(bf16)
        parts = []
        for p in range(spans):
            rows = slice(p * span, (p + 1) * span)
            q, k, v = qkv[r, 0, rows, :], qkv[r, 1, rows, :], qkv[r, 2, rows, :]
            dq = jnp.zeros((span, hc), f32)
            dk, dv = dq, dq
            for h in range(heads):
                mask = head_mask(span, hc, h)
                pr = prob[(r * spans + p) * heads + h]
                dc = d_ctx[rows] * mask
                dv = dv + dot_tn(pr.astype(bf16), dc)
                dp = dot_nt(dc, v)
                ds = (pr * (dp - jnp.sum(pr * dp, axis=1, keepdims=True))).astype(bf16)
                dq = dq + dot(ds, k * mask)
                dk = dk + dot_tn(ds, q * mask)
            scale = HEAD_DIM ** (-0.5)
            parts.append(((dq * scale).astype(bf16), (dk * scale).astype(bf16), dv.astype(bf16)))
        dq, dk, dv = (jnp.concatenate([part[i] for part in parts], axis=0) for i in range(3))
        head_out[r : r + 1, :] = jnp.sum(dq.astype(f32), axis=0, keepdims=True)
        head_out[4 + r : 5 + r, :] = jnp.sum(dv.astype(f32), axis=0, keepdims=True)
        d_mixed = jnp.concatenate([dq, dk, dv], axis=1)
        dres[...] += dot_nt(d_mixed, a[0:width, 0 : 3 * hc])
        out = send_out if r % 2 else keep_out
        out[r // 2] = jnp.concatenate(
            [dot(x_t, d_mixed), dot(d_att_t, ctx[r])], axis=1
        ).astype(bf16)
    slots = slot_out.shape[0]
    hot = (lax.broadcasted_iota(jnp.int32, (slots, tok), 0) == pos[...]).astype(bf16)
    slot_out[...] = dot(hot, dres[...].astype(bf16)).astype(bf16)


def call(kernel, outs, *args, scratch=()):
    whole = pl.BlockSpec(memory_space=pltpu.VMEM)
    return pl.pallas_call(
        kernel,
        out_shape=[jax.ShapeDtypeStruct(*o) for o in outs],
        in_specs=[whole] * len(args),
        out_specs=[whole] * len(outs),
        scratch_shapes=[pltpu.VMEM(*s) for s in scratch],
        compiler_params=pltpu.CompilerParams(vmem_limit_bytes=VMEM_LIMIT),
    )(*args)


def swap(v, axis, bit):
    size = lax.axis_size(axis)
    return lax.ppermute(v, axis, [(i, i ^ bit) for i in range(size)])


def add_low(a, b):
    return (a.astype(f32) + b.astype(f32)).astype(bf16)


def sum_over_dp(v):
    n_dp = lax.axis_size("dp")
    index = lax.axis_index("dp")
    rows = v.shape[0] // n_dp
    cur = v.reshape((n_dp, rows) + v.shape[1:])
    bit = 1
    while bit < n_dp:
        cur = cur.reshape((cur.shape[0] // 2, 2) + cur.shape[1:])
        mine = (index // bit) % 2
        keep = lax.dynamic_index_in_dim(cur, mine, 1, keepdims=False)
        send = lax.dynamic_index_in_dim(cur, 1 - mine, 1, keepdims=False)
        cur = add_low(keep, swap(send, "dp", bit))
        bit *= 2
    return cur[0]


def on_device(
    token_ids,
    pair_index,
    table,
    query_key_value_weight,
    b_q,
    b_v,
    attention_output_weight,
    b_o,
    ln1_gain,
    ln1_bias,
    feed_input_weight,
    feed_input_bias,
    feed_output_weight,
    b_out,
    ln2_gain,
    ln2_bias,
    grad_out,
):
    sent, seq = token_ids.shape
    tok = sent * seq
    rows_shard, width = table.shape
    shards = lax.axis_size(("dp", "mp"))
    n_mp = lax.axis_size("mp")
    capacity = 2 * tok // shards
    slots = shards * capacity
    hc = query_key_value_weight.shape[2]
    cols = feed_input_weight.shape[1]
    heads = hc // HEAD_DIM
    spans = tok // (2 * seq)

    bias_rows = jnp.zeros((16, width), bf16)
    bias_rows = bias_rows.at[0, 0:hc].set(b_q).at[0, hc : 2 * hc].set(b_v)
    bias_rows = bias_rows.at[1, 0:cols].set(feed_input_bias)
    own_a = jnp.concatenate(
        [
            jnp.concatenate(
                [query_key_value_weight.reshape(width, 3 * hc), attention_output_weight.T], axis=1
            ),
            bias_rows,
        ],
        axis=0,
    )
    own_f = jnp.concatenate([feed_input_weight, feed_output_weight], axis=0)
    a_x = swap(own_a, "mp", 2)
    f_x = swap(own_f, "mp", 2)
    a_all = (own_a, swap(own_a, "mp", 1), a_x, swap(a_x, "mp", 1))
    f_all = (own_f, swap(own_f, "mp", 1), f_x, swap(f_x, "mp", 1))

    flat_ids = token_ids.reshape(tok)
    owners = flat_ids // rows_shard
    within = flat_ids - owners * rows_shard
    order = jnp.arange(tok, dtype=jnp.int32)
    earlier = (owners[:, None] == owners[None, :]) & (order[None, :] < order[:, None])
    pos = owners * capacity + jnp.sum(earlier.astype(jnp.int32), axis=1)
    hit = jnp.arange(slots, dtype=jnp.int32)[:, None] == pos[None, :]
    requests = jnp.sum(jnp.where(hit, within[None, :] + 1, 0), axis=1) - 1
    requests = requests.reshape(shards, capacity)
    asked = lax.all_to_all(requests, ("dp", "mp"), split_axis=0, concat_axis=0, tiled=True)
    picked = jnp.take(table, jnp.maximum(asked, 0), axis=0)
    fetched = lax.all_to_all(picked, ("dp", "mp"), split_axis=0, concat_axis=0, tiled=True)

    vec = jnp.stack([b_o, ln1_gain, ln1_bias, b_out, ln2_gain, ln2_bias, b_o, b_o]).astype(f32)
    x, qkv, prob, ctx, norm1, inv1, biases = call(
        functools.partial(front_kernel, seq),
        [
            ((tok, width), bf16),
            ((n_mp, 3, tok, hc), bf16),
            ((n_mp * spans * heads, 2 * seq, 2 * seq), f32),
            ((n_mp, tok, hc), bf16),
            ((tok, width), f32),
            ((tok, 1), f32),
            ((n_mp, width), f32),
        ],
        fetched.reshape(slots, width),
        pos[:, None],
        *a_all,
        vec,
    )
    h, act, slope, hidden, norm2, inv2, cls, pooled = call(
        functools.partial(ffn_kernel, seq),
        [
            ((tok, width), bf16),
            ((n_mp, tok, cols), bf16),
            ((n_mp, tok, cols), f32),
            ((tok, width), f32),
            ((tok, width), f32),
            ((tok, 1), f32),
            ((sent, width), f32),
            ((sent, width), bf16),
        ],
        norm1,
        vec,
        *f_all,
        biases,
        scratch=[
            ((tok, width), f32),
            ((tok, width), bf16),
            ((tok, cols), f32),
            ((tok, width), f32),
        ],
    )
    everyone = jnp.broadcast_to(pooled[None], (shards, sent, width))
    all_pooled = lax.all_to_all(
        everyone, ("dp", "mp"), split_axis=0, concat_axis=0, tiled=True
    ).reshape(shards * sent, width)
    own_start = lax.axis_index(("dp", "mp")) * sent
    loss, d_first, keep_f, send_f, sums2 = call(
        functools.partial(back_ffn_kernel, seq),
        [
            ((1, 1), f32),
            ((tok, width), f32),
            ((2, 2, width, cols), bf16),
            ((2, 2, width, cols), bf16),
            ((8, width), f32),
        ],
        all_pooled,
        pair_index,
        pair_index.T - own_start,
        cls,
        grad_out.reshape(tok, width),
        norm2,
        inv2,
        vec,
        h,
        act,
        slope,
        *f_all,
        scratch=[
            ((tok, width), f32),
            ((tok, width), bf16),
            ((tok, cols), bf16),
            ((tok, cols), f32),
        ],
    )
    keep_a, send_a, outgoing_rows, sums1, head_sums = call(
        functools.partial(back_attend_kernel, seq),
        [
            ((2, width, 4 * hc), bf16),
            ((2, width, 4 * hc), bf16),
            ((slots, width), bf16),
            ((8, width), f32),
            ((8, hc), f32),
        ],
        d_first,
        norm1,
        inv1,
        vec,
        x,
        qkv,
        prob,
        ctx,
        pos[None, :],
        *a_all,
        scratch=[((tok, width), bf16), ((tok, width), f32)],
    )

    half_f = add_low(keep_f, swap(send_f, "mp", 1))
    half_a = add_low(keep_a, swap(send_a, "mp", 1))
    full_in = add_low(half_f[0, 0], swap(half_f[1, 0], "mp", 2))
    full_out = add_low(half_f[0, 1], swap(half_f[1, 1], "mp", 2))
    full_a = add_low(half_a[0], swap(half_a[1], "mp", 2))
    in_part = sum_over_dp(full_in).astype(f32)
    out_part = sum_over_dp(full_out).astype(f32).T
    part_a = sum_over_dp(full_a).astype(f32)
    qkv_part = part_a[:, : 3 * hc].reshape(-1, 3, hc)
    o_part = part_a[:, 3 * hc :].T

    share_cols = width // shards
    ffn_share = cols * n_mp // shards
    turn = jnp.arange(n_mp, dtype=jnp.int32) ^ lax.axis_index("mp")
    shared = jnp.concatenate(
        [
            sums1[0:3],
            sums2[0:3],
            head_sums[0:4][turn].reshape(1, width),
            head_sums[4:8][turn].reshape(1, width),
        ],
        axis=0,
    )
    outgoing = jnp.concatenate(
        [
            shared.reshape(8, shards, share_cols).transpose(1, 0, 2).reshape(shards, -1),
            sums2[3:7][turn].reshape(shards, ffn_share),
        ],
        axis=1,
    )
    arrived = lax.all_to_all(
        outgoing_rows.reshape(shards, capacity, width),
        ("dp", "mp"), split_axis=0, concat_axis=0, tiled=True,
    ).astype(f32)
    collected = lax.all_to_all(
        outgoing.astype(bf16), ("dp", "mp"), split_axis=0, concat_axis=0, tiled=True
    ).astype(f32)
    live_mask = (asked >= 0).astype(f32)[:, :, None]
    table_grad = (
        jnp.zeros((rows_shard, width), f32)
        .at[jnp.maximum(asked, 0)]
        .add(arrived * live_mask)
    )
    totals = jnp.sum(collected, axis=0)
    shared_sum = totals[: 8 * share_cols].reshape(8, share_cols)
    ffn_sum = totals[8 * share_cols :]
    return (
        hidden.reshape(sent, seq, width),
        loss[0, 0],
        table_grad,
        qkv_part,
        shared_sum[6],
        shared_sum[7],
        o_part,
        shared_sum[0],
        shared_sum[1],
        shared_sum[2],
        in_part,
        ffn_sum,
        out_part,
        shared_sum[3],
        shared_sum[4],
        shared_sum[5],
    )


def solution(mesh):
    in_specs = (
        P(("dp", "mp"), None),
        P(),
        P(("dp", "mp"), None),
        P(None, None, "mp"),
        P("mp"),
        P("mp"),
        P("mp", None),
        P(),
        P(),
        P(),
        P(None, "mp"),
        P("mp"),
        P("mp", None),
        P(),
        P(),
        P(),
        P(("dp", "mp"), None, None),
    )
    out_specs = (
        P(("dp", "mp"), None, None),
        P(),
        P(("dp", "mp"), None),
        P("dp", None, "mp"),
        P(("dp", "mp")),
        P(("dp", "mp")),
        P("mp", "dp"),
        P(("dp", "mp")),
        P(("dp", "mp")),
        P(("dp", "mp")),
        P("dp", "mp"),
        P(("dp", "mp")),
        P("mp", "dp"),
        P(("dp", "mp")),
        P(("dp", "mp")),
        P(("dp", "mp")),
    )
    return jax.shard_map(
        on_device, mesh=mesh, in_specs=in_specs, out_specs=out_specs, check_vma=False
    )
```

time: 748 us -> 364 us (0.49)
  waiting for transfers between devices: 416 us -> 147 us
  Pallas kernels: 0 us -> 58.9 us
  matrix products: 57.3 us -> 0 us
  blocking collectives: 80.3 us -> 26.1 us
  local copies, waits for them, and re-layouts: 88.9 us -> 38.2 us
  starting transfers between devices: 12 us -> 37.3 us
  other arithmetic: 68 us -> 49.1 us
  between operations: 18.2 us -> 1.52 us
    reduce_scatter x7 -> x0, waiting for transfers between devices: 282 us -> none  [the longest x1 64.8 us: on_device(): lax.psum_scatter(grad_w_in.astype(jnp.bfloat16), 'dp', scatter_dimension=...]
    ppermute x0 -> x20, waiting for transfers between devices: none -> 102 us  [swap(): return lax.ppermute(v, axis, [(i, i ^ bit) for i in range(size)])]
    all_gather x4 -> x0, waiting for transfers between devices: 72 us -> none  [the longest x1 19.5 us: on_device(): d_att_group = lax.all_gather(d_att, 'mp', axis=0, tiled=True)]
    unnamed x13 -> x0, waiting for transfers between devices: 61.3 us -> none
    pallas_call x0 -> x4, Pallas kernels: none -> 58.9 us  [call(): pl.pallas_call(kernel, out_shape=[jax.ShapeDtypeStruct(*o) for o in outs]...]
    dot_general x21 -> x0, matrix products: 57.3 us -> none  [the longest x1 10.1 us: ffn_front(): jnp.dot(h_group, feed_input_weight, preferred_element_type=jnp.float32)]
    all_to_all x2 -> x4, waiting for transfers between devices: 0.01 us -> 44.7 us  [the longest x1 20 us: on_device(): lax.all_to_all(outgoing.astype(bf16), ('dp', 'mp'), split_axis=0, concat_...]
    all_gather x1 -> x0, blocking collectives: 43.7 us -> none  [on_device(): all_pooled = lax.all_gather(pooled, ('dp', 'mp'), axis=0, tiled=True)]
  transfers between devices with their start and end apart: 14 -> 24, of which waited for: 11 -> 12; matrix products, arithmetic and copies ran while one was open for 8% -> 22% of each run, Pallas kernels for 0% -> 7%
where the time goes in v1:
time: 364 us; the launch traced here: 358 us
  waiting for transfers between devices  147 us (40%)
  Pallas kernels  58.9 us (16%)
  other arithmetic  49.1 us (13%)
  local copies, waits for them, and re-layouts  38.2 us (10%)
  starting transfers between devices  37.3 us (10%)
  blocking collectives  26.1 us (7%)
    ppermute x20, waiting for transfers between devices, swap(): return lax.ppermute(v, axis, [(i, i ^ bit) for i in range(size)])  102 us
    pallas_call x4, Pallas kernels, call(): pl.pallas_call(kernel, out_shape=[jax.ShapeDtypeStruct(*o) for o in outs]...  58.9 us
    all_to_all x1, blocking collectives, on_device(): lax.all_to_all(requests, ('dp', 'mp'), split_axis=0, concat_axis=0, tiled...  26.1 us
    scatter-add x1, other arithmetic, on_device(): table_grad = jnp.zeros((rows_shard, width), f32).at[jnp.maximum(asked, 0)...  23.4 us
    ppermute x20, starting transfers between devices, swap(): return lax.ppermute(v, axis, [(i, i ^ bit) for i in range(size)])  22.3 us
    all_to_all x1, waiting for transfers between devices, on_device(): lax.all_to_all(outgoing.astype(bf16), ('dp', 'mp'), split_axis=0, concat_...  20 us
    all_to_all x1, waiting for transfers between devices, on_device(): lax.all_to_all(picked, ('dp', 'mp'), split_axis=0, concat_axis=0, tiled=T...  17.3 us
    convert_element_type x10, other arithmetic, add_low(): return (a.astype(f32) + b.astype(f32)).astype(bf16)  14.3 us
  transfers between devices with their start and end apart: 24, of which 12 were waited for; matrix products, arithmetic and copies ran while one was open for 22% of the time, Pallas kernels for 7%

profile of v1, /device:TPU:0, one launch (start us, length us, event | category | flops | bytes accessed | tf_op | source)
XLA Modules:
  0.0 358.2 jit_solution(2298043736064723361)
XLA Ops:
  0.7 1.4 constant_dynamic-update-slice_fusion.1
  2.4 3.0 collective-permute-start.4
  5.4 0.9 copy.118
  6.4 1.5 copy.119
  9.2 2.0 broadcast_select_fusion.1
  11.2 1.7 scatter.11
  12.9 2.2 pad_maximum_fusion.a0
  15.2 0.8 collective-permute-start.1
  16.4 41.2 %collective-permute-done.4.f2 = bf16[1536,768]{1,0:T(8,128)(2,1)} collective-permute-done((bf16[1536,768]{1,0:T(8,128)(2,1)S(1)}, bf16[1536,768]{1,0:T(8,128)(2,1)}, u32[]{:S(2)}, u32[]{:S(2)}) %collective-permute-start.4) | collective-permute-done | bytes 2359328 | tf_op jit(solution)/shard_map/ppermute | solution.py:325
  57.7 26.1 %all_to_all.27 = s32[32,1,16]{2,1,0:T(1,128)S(1)} all-to-all(s32[32,1,16]{2,1,0:T(1,128)S(1)} %bitcast.129), channel_id=1, replica_groups=mesh['dp'=8,'mp'=4] {'dp','mp'}, dimensions={0} | all-to-all | bytes 4096 | tf_op jit(solution)/shard_map/all_to_all | solution.py:406
  84.2 13.3 %gather_fusion = bf16[512,768]{1,0:T(8,128)(2,1)S(1)} fusion(bf16[15664,768]{1,0:T(8,128)(2,1)} %param.25, s32[1024]{0:T(1024)S(1)} %pad_clamp_fusion.1), kind=kCustom, calls=%fused_computation | custom fusion | bytes 1574912 | tf_op jit(solution)/shard_map/jit(_take)/gather | solution.py:407
  97.6 1.0 broadcast_select_fusion
  98.6 5.2 %all-to-all-start.1 = ((bf16[32,16,768]{2,1,0:T(8,128)(2,1)}), bf16[32,16,768]{2,1,0:T(8,128)(2,1)S(1)}, u32[]{:S(2)}, u32[]{:S(2)}) async-start(bf16[32,16,768]{2,1,0:T(8,128)(2,1)} %broadcast_select_fusion), calls=%async_computation.1 | async-start | bytes 1572864 | tf_op jit(solution)/shard_map/all_to_all | solution.py:408
  105.7 0.7 fusion.18.pos
  106.4 0.7 collective-permute-done.a1
  107.1 17.3 %all-to-all-done.1 = bf16[32,16,768]{2,1,0:T(8,128)(2,1)S(1)} async-done(((bf16[32,16,768]{2,1,0:T(8,128)(2,1)}), bf16[32,16,768]{2,1,0:T(8,128)(2,1)S(1)}, u32[]{:S(2)}, u32[]{:S(2)}) %all-to-all-start.1) | async-done | bytes 786464 | tf_op jit(solution)/shard_map/all_to_all | solution.py:408
  124.4 0.9 copy-done.2
  125.3 9.9 %shard_map.288 = (bf16[256,768]{1,0:T(8,128)(2,1)}, bf16[4,3,256,192]{3,2,1,0:T(8,128)(2,1)}, f32[24,128,128]{2,1,0:T(8,128)}, bf16[4,256,192]{2,1,0:T(8,128)(2,...) custom-call(bf16[512,768]{1,0:T(8,128)(2,1)} %bitcast.116, s32[256,1]{1,0:T(8,128)} %fusion.18.pos, ...), custom_call_target="tpu_custom_call" | custom-call | tf_op jit(solution)/shard_map/pallas_call | solution.py:313
  135.3 13.6 %shard_map.289 = (bf16[256,768]{1,0:T(8,128)(2,1)}, bf16[4,256,768]{2,1,0:T(8,128)(2,1)}, f32[4,256,768]{2,1,0:T(8,128)}, f32[256,768]{1,0:T(8,128)}, f32[256,76...) custom-call(f32[256,768]{1,0:T(8,128)} %get-tuple-element.77.norm1, ...), custom_call_target="tpu_custom_call" | custom-call | tf_op jit(solution)/shard_map/pallas_call | solution.py:313
  148.9 1.4 broadcast_in_dim.30
  150.3 3.9 %all-to-all-start.2 = ((bf16[32,4,768]{2,1,0:T(4,128)(2,1)}), bf16[32,4,768]{2,1,0:T(4,128)(2,1)S(1)}, u32[]{:S(2)}, u32[]{:S(2)}) async-start(bf16[32,4,768]{2,1,0:T(4,128)(2,1)} %broadcast_in_dim.30), calls=%async_computation.2 | async-start | bytes 393216 | tf_op jit(solution)/shard_map/all_to_all | solution.py:451
  154.4 0.7 copy.120.pair
  155.7 7.4 %all-to-all-done.2 = bf16[32,4,768]{2,1,0:T(4,128)(2,1)S(1)} async-done(((bf16[32,4,768]{2,1,0:T(4,128)(2,1)}), bf16[32,4,768]{2,1,0:T(4,128)(2,1)S(1)}, u32[]{:S(2)}, u32[]{:S(2)}) %all-to-all-start.2) | async-done | bytes 196640 | tf_op jit(solution)/shard_map/all_to_all | solution.py:451
  163.1 0.7 reshape.497.pooled
  163.8 18.6 %shard_map.290 = (f32[1,1]{1,0:T(1,128)}, f32[256,768]{1,0:T(8,128)}, bf16[2,2,768,768]{3,2,1,0:T(8,128)(2,1)}, bf16[2,2,768,768]{3,2,1,0:T(8,128)(2,1)}, f32[8,768]{1,0:T(8,128)}) custom-call(bf16[128,768]{1,0:T(8,128)(2,1)} %reshape.497.pooled, s32[64,2]{1,0:T(8,128)} %copy.120.pair, s32[2,64]{1,0:T(2,128)} %subtract_bitcast_fusion.pair_own, ...), custom_call_target="tpu_custom_call" | custom-call | tf_op jit(solution)/shard_map/pallas_call | solution.py:313
  183.5 16.8 %shard_map.291 = (bf16[2,768,768]{2,1,0:T(8,128)(2,1)}, bf16[2,768,768]{2,1,0:T(8,128)(2,1)}, bf16[512,768]{1,0:T(8,128)(2,1)}, f32[8,768]{1,0:T(8,128)}, f32[8,192]{1,0:T(8,128)}) custom-call(f32[256,768]{1,0:T(8,128)} %get-tuple-element.88.dfirst, f32[256,768]{1,0:T(8,128)} %get-tuple-element.77.norm1, f32[256,1]{1,0:T(8,128)} %get-tuple-element.89.inv1, ...), custom_call_target="tpu_custom_call" | custom-call | tf_op jit(solution)/shard_map/pallas_call | solution.py:313
  200.3 4.7 %collective-permute-done.6 = bf16[2,768,768]{2,1,0:T(8,128)(2,1)S(1)} collective-permute-done((bf16[2,768,768]{2,1,0:T(8,128)(2,1)}, bf16[2,768,768]{2,1,0:T(8,128)(2,1)S(1)}, u32[]{:S(2)}, u32[]{:S(2)}) %collective-permute-start.6) | collective-permute-done | bytes 2359328 | tf_op jit(solution)/shard_map/ppermute | solution.py:325
  205.1 2.2 add_convert_fusion.1
  207.3 1.1 slice_bitcast_fusion.4
  210.2 0.8 slice.196
  213.3 0.7 reshape.564
  214.0 3.0 all-to-all-start.4
  217.1 20.0 %all-to-all-done.4 = bf16[32,2,144]{2,1,0:T(2,128)(2,1)S(1)} async-done(((bf16[32,2,144]{2,1,0:T(2,128)(2,1)}), bf16[32,2,144]{2,1,0:T(2,128)(2,1)S(1)}, u32[]{:S(2)}, u32[]{:S(2)}) %all-to-all-start.4) | async-done | bytes 18464 | tf_op jit(solution)/shard_map/all_to_all | solution.py:539
  237.1 2.9 all-to-all-start.3
  240.2 1.6 fusion.4
  241.8 1.9 collective-permute-start.8
  243.7 4.9 %add_convert_fusion = bf16[2,2,768,768]{3,2,1,0:T(8,128)(2,1)S(1)} fusion(bf16[2,2,768,768]{3,2,1,0:T(8,128)(2,1)} %collective-permute-done.11, bf16[2,2,768,768]{3,2,1,0:T(8,128)(2,1)} %get-tuple-element.100), kind=kLoop, calls=%fused_computation.7 | loop fusion | flops 9437184 | bytes 14155776 | tf_op jit(solution)/shard_map/convert_element_type | solution.py:329
  248.6 1.7 slice_bitcast_fusion
  250.3 1.3 copy-done
  251.6 1.5 collective-permute-start.16
  253.6 10.4 %collective-permute-done.8 = bf16[4,96,768]{2,1,0:T(8,128)(2,1)S(1)} collective-permute-done((bf16[4,96,768]{2,1,0:T(8,128)(2,1)S(1)}, bf16[4,96,768]{2,1,0:T(8,128)(2,1)S(1)}, u32[]{:S(2)}, u32[]{:S(2)}) %collective-permute-start.8) | collective-permute-done | bytes 589856 | tf_op jit(solution)/shard_map/ppermute | solution.py:325
  264.2 0.7 dynamic-slice_bitcast_fusion.5
  264.9 1.7 collective-permute-start.9
  268.1 23.4 %scatter_custom_fusion = f32[15664,768]{1,0:T(8,128)} fusion(s32[512]{0:T(512)S(1)} %reshape.519, f32[512,768]{1,0:T(8,128)S(1)} %bitcast.123, f32[]{:T(128)} %constant.242.clone.1), kind=kCustom, calls=%fused_computation.5 | custom fusion | flops 393216 | bytes 48119812 | tf_op jit(solution)/shard_map/scatter-add | solution.py:546
  291.6 2.2 collective-permute-start.10
  293.7 12.7 %collective-permute-done.12 = bf16[768,768]{1,0:T(8,128)(2,1)} collective-permute-done((bf16[768,768]{1,0:T(8,128)(2,1)}, bf16[768,768]{1,0:T(8,128)(2,1)}, u32[]{:S(2)}, u32[]{:S(2)}) %collective-permute-start.12) | collective-permute-done | bytes 1179680 | tf_op jit(solution)/shard_map/ppermute | solution.py:325
  306.4 2.9 fusion.2
  309.4 0.7 collective-permute-start.17
  310.1 0.9 dynamic-slice_bitcast_fusion.1
  311.0 1.4 collective-permute-start.13
  312.5 0.7 copy.130
  313.4 0.9 copy.129
  314.3 11.5 %collective-permute-done.17 = bf16[4,96,768]{2,1,0:T(8,128)(2,1)} collective-permute-done((bf16[4,96,768]{2,1,0:T(8,128)(2,1)S(1)}, bf16[4,96,768]{2,1,0:T(8,128)(2,1)}, u32[]{:S(2)}, u32[]{:S(2)}) %collective-permute-start.17) | collective-permute-done | bytes 589856 | tf_op jit(solution)/shard_map/ppermute | solution.py:325
  325.8 1.2 fusion.5
  327.1 1.6 collective-permute-start.18
  328.7 8.2 %collective-permute-done.13 = bf16[4,96,768]{2,1,0:T(8,128)(2,1)} collective-permute-done((bf16[4,96,768]{2,1,0:T(8,128)(2,1)}, bf16[4,96,768]{2,1,0:T(8,128)(2,1)}, u32[]{:S(2)}, u32[]{:S(2)}) %collective-permute-start.13) | collective-permute-done | bytes 589856 | tf_op jit(solution)/shard_map/ppermute | solution.py:325
  336.9 1.2 fusion.6
  338.1 1.7 collective-permute-start.14
  339.9 1.6 collective-permute-start.19
  341.5 7.2 %collective-permute-done.14 = bf16[2,96,768]{2,1,0:T(8,128)(2,1)S(1)} collective-permute-done((bf16[2,96,768]{2,1,0:T(8,128)(2,1)S(1)}, bf16[2,96,768]{2,1,0:T(8,128)(2,1)S(1)}, u32[]{:S(2)}, u32[]{:S(2)}) %collective-permute-start.14) | collective-permute-done | bytes 294944 | tf_op jit(solution)/shard_map/ppermute | solution.py:325
  348.9 2.0 collective-permute-start.15
  350.9 0.7 convert_bitcast_fusion
  351.6 5.6 %collective-permute-done.15 = bf16[1,96,768]{2,1,0:T(8,128)(2,1)S(1)} collective-permute-done((bf16[1,96,768]{2,1,0:T(8,128)(2,1)S(1)}, bf16[1,96,768]{2,1,0:T(8,128)(2,1)S(1)}, u32[]{:S(2)}, u32[]{:S(2)}) %collective-permute-start.15) | collective-permute-done | bytes 147488 | tf_op jit(solution)/shard_map/ppermute | solution.py:325
  357.3 0.7 fusion.15
  (135 shorter events, 13.3 us)
Async XLA Ops:
  0.6 1.6 copy-start.3
  2.3 3.1 copy-start.17
  2.3 3.1 copy-start.9
  2.3 3.2 copy-start.4
  2.4 12.8 %copy-start.1 = (bf16[1536,768]{1,0:T(8,128)(2,1)}, bf16[1536,768]{1,0:T(8,128)(2,1)S(1)}, u32[]{:S(2)}) copy-start(bf16[1536,768]{1,0:T(8,128)(2,1)S(1)} %constant_dynamic-update-slice_fusion.f0) | copy-start | bytes 7077892
  2.4 6.2 %copy-start.18 = (s32[2]{0:T(128)S(1)}, s32[2]{0:T(128)}, u32[]{:S(2)}) copy-start(s32[2]{0:T(128)} %constant.236.clone.1) | copy-start | bytes 28
  2.4 6.8 %copy-start.16 = (bf16[192]{0:T(256)(128)(2,1)S(1)}, bf16[192]{0:T(256)(128)(2,1)}, u32[]{:S(2)}) copy-start(bf16[192]{0:T(256)(128)(2,1)} %param.28) | copy-start | bytes 1156
  2.4 55.2 %collective-permute-start.4 = (bf16[1536,768]{1,0:T(8,128)(2,1)S(1)}, bf16[1536,768]{1,0:T(8,128)(2,1)}, u32[]{:S(2)}, u32[]{:S(2)}) collective-permute-start(bf16[1536,768]{1,0:T(8,128)(2,1)S(1)} %constant_dynamic-update-slice_fusion.f0), channel_id=1, source_target_pairs={{0,2},{1,3},{2,0},{3,1},{4,6},{5,7},{6,4},{7,5},{8,10},{9,11},{10,... | collective-permute-start | bytes 7077896 | tf_op jit(solution)/shard_map/ppermute | solution.py:325
  5.4 129.8 %collective-permute-start.3 = (bf16[1536,768]{1,0:T(8,128)(2,1)S(1)}, bf16[1536,768]{1,0:T(8,128)(2,1)}, u32[]{:S(2)}, u32[]{:S(2)}) collective-permute-start(bf16[1536,768]{1,0:T(8,128)(2,1)S(1)} %constant_dynamic-update-slice_fusion.f0), channel_id=1, source_target_pairs={{0,1},{1,0},{2,3},{3,2},{4,5},{5,4},{6,7},{7,6},{8,9},{9,8},{10,11... | collective-permute-start | bytes 7077896 | tf_op jit(solution)/shard_map/ppermute | solution.py:325
  7.9 8.1 %copy-start.5 = (s32[4,64]{1,0:T(4,128)S(1)}, s32[4,64]{1,0:T(4,128)}, u32[]{:S(2)}) copy-start(s32[4,64]{1,0:T(4,128)} %param.23) | copy-start | bytes 3076
  15.2 89.1 %collective-permute-start.1 = (bf16[784,768]{1,0:T(8,128)(2,1)}, bf16[784,768]{1,0:T(8,128)(2,1)}, u32[]{:S(2)}, u32[]{:S(2)}) collective-permute-start(bf16[784,768]{1,0:T(8,128)(2,1)} %pad_maximum_fusion.a0), channel_id=1, source_target_pairs={{0,2},{1,3},{2,0},{3,1},{4,6},{5,7},{6,4},{7,5},{8,10},{9,11},{10,... | collective-permute-start | bytes 3612680 | tf_op jit(solution)/shard_map/ppermute | solution.py:325
  57.6 77.7 %collective-permute-start.5 = (bf16[1536,768]{1,0:T(8,128)(2,1)}, bf16[1536,768]{1,0:T(8,128)(2,1)}, u32[]{:S(2)}, u32[]{:S(2)}) collective-permute-start(bf16[1536,768]{1,0:T(8,128)(2,1)} %collective-permute-done.4.f2), channel_id=1, source_target_pairs={{0,1},{1,0},{2,3},{3,2},{4,5},{5,4},{6,7},{7,6},{8,9},{9,8},{10,11... | collective-permute-start | bytes 7077896 | tf_op jit(solution)/shard_map/ppermute | solution.py:325
  97.5 6.9 %copy-start.10 = (bf16[768]{0:T(1024)(128)(2,1)S(1)}, bf16[768]{0:T(1024)(128)(2,1)}, u32[]{:S(2)}) copy-start(bf16[768]{0:T(1024)(128)(2,1)} %param.30) | copy-start | bytes 4612
  97.5 6.9 %copy-start.11 = (bf16[768]{0:T(1024)(128)(2,1)S(1)}, bf16[768]{0:T(1024)(128)(2,1)}, u32[]{:S(2)}) copy-start(bf16[768]{0:T(1024)(128)(2,1)} %param.31) | copy-start | bytes 4612
  97.5 6.9 %copy-start.12 = (bf16[768]{0:T(1024)(128)(2,1)S(1)}, bf16[768]{0:T(1024)(128)(2,1)}, u32[]{:S(2)}) copy-start(bf16[768]{0:T(1024)(128)(2,1)} %param.32) | copy-start | bytes 4612
  97.5 6.9 %copy-start.13 = (bf16[768]{0:T(1024)(128)(2,1)S(1)}, bf16[768]{0:T(1024)(128)(2,1)}, u32[]{:S(2)}) copy-start(bf16[768]{0:T(1024)(128)(2,1)} %param.36) | copy-start | bytes 4612
  97.5 6.9 %copy-start.14 = (bf16[768]{0:T(1024)(128)(2,1)S(1)}, bf16[768]{0:T(1024)(128)(2,1)}, u32[]{:S(2)}) copy-start(bf16[768]{0:T(1024)(128)(2,1)} %param.37) | copy-start | bytes 4612
  97.6 6.9 %copy-start.15 = (bf16[768]{0:T(1024)(128)(2,1)S(1)}, bf16[768]{0:T(1024)(128)(2,1)}, u32[]{:S(2)}) copy-start(bf16[768]{0:T(1024)(128)(2,1)} %param.38) | copy-start | bytes 4612
  98.6 25.8 %all-to-all-start.1 = ((bf16[32,16,768]{2,1,0:T(8,128)(2,1)}), bf16[32,16,768]{2,1,0:T(8,128)(2,1)S(1)}, u32[]{:S(2)}, u32[]{:S(2)}) async-start(bf16[32,16,768]{2,1,0:T(8,128)(2,1)} %broadcast_select_fusion), calls=%async_computation.1 | async-start | bytes 1572864 | tf_op jit(solution)/shard_map/all_to_all | solution.py:408
  103.8 3.3 collective-permute-start
  104.2 20.2 %collective-permute-start.2 = (bf16[784,768]{1,0:T(8,128)(2,1)}, bf16[784,768]{1,0:T(8,128)(2,1)}, u32[]{:S(2)}, u32[]{:S(2)}) collective-permute-start(bf16[784,768]{1,0:T(8,128)(2,1)} %collective-permute-done.1.a2), channel_id=1, source_target_pairs={{0,1},{1,0},{2,3},{3,2},{4,5},{5,4},{6,7},{7,6},{8,9},{9,8},{10,11... | collective-permute-start | bytes 3612680 | tf_op jit(solution)/shard_map/ppermute | solution.py:325
  124.4 0.9 copy-start.2
  135.3 19.1 %copy-start.7 = (s32[64,2]{0,1:T(2,128)S(1)}, s32[64,2]{0,1:T(2,128)}, u32[]{:S(2)}) copy-start(s32[64,2]{0,1:T(2,128)} %param.24) | copy-start | bytes 1540
  150.3 12.8 %all-to-all-start.2 = ((bf16[32,4,768]{2,1,0:T(4,128)(2,1)}), bf16[32,4,768]{2,1,0:T(4,128)(2,1)S(1)}, u32[]{:S(2)}, u32[]{:S(2)}) async-start(bf16[32,4,768]{2,1,0:T(4,128)(2,1)} %broadcast_in_dim.30), calls=%async_computation.2 | async-start | bytes 393216 | tf_op jit(solution)/shard_map/all_to_all | solution.py:451
  182.4 61.4 %collective-permute-start.11 = (bf16[2,2,768,768]{3,2,1,0:T(8,128)(2,1)}, bf16[2,2,768,768]{3,2,1,0:T(8,128)(2,1)}, u32[]{:S(2)}, u32[]{:S(2)}) collective-permute-start(bf16[2,2,768,768]{3,2,1,0:T(8,128)(2,1)} %get-tuple-element.101), channel_id=1, source_target_pairs={{0,1},{1,0},{2,3},{3,2},{4,5},{5,4},{6,7},{7,6},{8,9},{9,8},{10,11... | collective-permute-start | bytes 14155784 | tf_op jit(solution)/shard_map/ppermute | solution.py:325
  200.3 4.7 %collective-permute-start.6 = (bf16[2,768,768]{2,1,0:T(8,128)(2,1)}, bf16[2,768,768]{2,1,0:T(8,128)(2,1)S(1)}, u32[]{:S(2)}, u32[]{:S(2)}) collective-permute-start(bf16[2,768,768]{2,1,0:T(8,128)(2,1)} %get-tuple-element.96), channel_id=1, source_target_pairs={{0,1},{1,0},{2,3},{3,2},{4,5},{5,4},{6,7},{7,6},{8,9},{9,8},{10,11... | collective-permute-start | bytes 7077896 | tf_op jit(solution)/shard_map/ppermute | solution.py:325
  207.3 1.6 copy-start.6
  207.3 1.6 copy-start.8
  208.4 31.8 %collective-permute-start.7 = (bf16[768,768]{1,0:T(8,128)(2,1)}, bf16[768,768]{1,0:T(8,128)(2,1)}, u32[]{:S(2)}, u32[]{:S(2)}) collective-permute-start(bf16[768,768]{1,0:T(8,128)(2,1)} %slice_bitcast_fusion.4), channel_id=1, source_target_pairs={{0,2},{1,3},{2,0},{3,1},{4,6},{5,7},{6,4},{7,5},{8,10},{9,11},{10,... | collective-permute-start | bytes 3538952 | tf_op jit(solution)/shard_map/ppermute | solution.py:325
  214.0 23.1 %all-to-all-start.4 = ((bf16[32,2,144]{2,1,0:T(2,128)(2,1)}), bf16[32,2,144]{2,1,0:T(2,128)(2,1)S(1)}, u32[]{:S(2)}, u32[]{:S(2)}) async-start(bf16[32,2,144]{2,1,0:T(2,128)(2,1)} %reshape.564), calls=%async_computation.4 | async-start | bytes 65536 | tf_op jit(solution)/shard_map/all_to_all | solution.py:539
  237.1 30.7 %all-to-all-start.3 = ((bf16[32,16,768]{2,1,0:T(8,128)(2,1)}), bf16[32,16,768]{2,1,0:T(8,128)(2,1)S(1)}, u32[]{:S(2)}, u32[]{:S(2)}) async-start(bf16[32,16,768]{2,1,0:T(8,128)(2,1)} %bitcast.128), calls=%async_computation.3 | async-start | bytes 1572864 | tf_op jit(solution)/shard_map/all_to_all | solution.py:535
  241.8 22.2 %collective-permute-start.8 = (bf16[4,96,768]{2,1,0:T(8,128)(2,1)S(1)}, bf16[4,96,768]{2,1,0:T(8,128)(2,1)S(1)}, u32[]{:S(2)}, u32[]{:S(2)}) collective-permute-start(bf16[4,96,768]{2,1,0:T(8,128)(2,1)S(1)} %dynamic-slice_bitcast_fusion.2), channel_id=1, source_target_pairs={{0,4},{4,0},{8,12},{12,8},{16,20},{20,16},{24,28},{28,24},{1,5},{5... | collective-permute-start | bytes 1769480 | tf_op jit(solution)/shard_map/ppermute | solution.py:325
  248.6 3.0 copy-start
  251.6 42.1 %collective-permute-start.16 = (bf16[768,768]{1,0:T(8,128)(2,1)}, bf16[768,768]{1,0:T(8,128)(2,1)}, u32[]{:S(2)}, u32[]{:S(2)}) collective-permute-start(bf16[768,768]{1,0:T(8,128)(2,1)} %get-tuple-element.186), channel_id=1, source_target_pairs={{0,2},{1,3},{2,0},{3,1},{4,6},{5,7},{6,4},{7,5},{8,10},{9,11},{10,... | collective-permute-start | bytes 3538952 | tf_op jit(solution)/shard_map/ppermute | solution.py:325
  253.1 53.4 %collective-permute-start.12 = (bf16[768,768]{1,0:T(8,128)(2,1)}, bf16[768,768]{1,0:T(8,128)(2,1)}, u32[]{:S(2)}, u32[]{:S(2)}) collective-permute-start(bf16[768,768]{1,0:T(8,128)(2,1)} %get-tuple-element.187), channel_id=1, source_target_pairs={{0,2},{1,3},{2,0},{3,1},{4,6},{5,7},{6,4},{7,5},{8,10},{9,11},{10,... | collective-permute-start | bytes 3538952 | tf_op jit(solution)/shard_map/ppermute | solution.py:325
  264.9 26.5 %collective-permute-start.9 = (bf16[2,96,768]{2,1,0:T(8,128)(2,1)}, bf16[2,96,768]{2,1,0:T(8,128)(2,1)S(1)}, u32[]{:S(2)}, u32[]{:S(2)}) collective-permute-start(bf16[2,96,768]{2,1,0:T(8,128)(2,1)} %dynamic-slice_bitcast_fusion.5), channel_id=1, source_target_pairs={{0,8},{4,12},{8,0},{12,4},{16,24},{20,28},{24,16},{28,20},{1,9},{5... | collective-permute-start | bytes 884744 | tf_op jit(solution)/shard_map/ppermute | solution.py:325
  291.6 18.5 %collective-permute-start.10 = (bf16[1,96,768]{2,1,0:T(8,128)(2,1)S(1)}, bf16[1,96,768]{2,1,0:T(8,128)(2,1)S(1)}, u32[]{:S(2)}, u32[]{:S(2)}) collective-permute-start(bf16[1,96,768]{2,1,0:T(8,128)(2,1)S(1)} %constant_dynamic-slice_fusion.1), channel_id=1, source_target_pairs={{0,16},{4,20},{8,24},{12,28},{16,0},{20,4},{24,8},{28,12},{1,17},{... | collective-permute-start | bytes 442376 | tf_op jit(solution)/shard_map/ppermute | solution.py:325
  309.4 16.4 %collective-permute-start.17 = (bf16[4,96,768]{2,1,0:T(8,128)(2,1)S(1)}, bf16[4,96,768]{2,1,0:T(8,128)(2,1)}, u32[]{:S(2)}, u32[]{:S(2)}) collective-permute-start(bf16[4,96,768]{2,1,0:T(8,128)(2,1)S(1)} %dynamic-slice_bitcast_fusion), channel_id=1, source_target_pairs={{0,4},{4,0},{8,12},{12,8},{16,20},{20,16},{24,28},{28,24},{1,5},{5... | collective-permute-start | bytes 1769480 | tf_op jit(solution)/shard_map/ppermute | solution.py:325
  311.0 25.8 %collective-permute-start.13 = (bf16[4,96,768]{2,1,0:T(8,128)(2,1)}, bf16[4,96,768]{2,1,0:T(8,128)(2,1)}, u32[]{:S(2)}, u32[]{:S(2)}) collective-permute-start(bf16[4,96,768]{2,1,0:T(8,128)(2,1)} %dynamic-slice_bitcast_fusion.1), channel_id=1, source_target_pairs={{0,4},{4,0},{8,12},{12,8},{16,20},{20,16},{24,28},{28,24},{1,5},{5... | collective-permute-start | bytes 1769480 | tf_op jit(solution)/shard_map/ppermute | solution.py:325
  327.1 12.7 %collective-permute-start.18 = (bf16[2,96,768]{2,1,0:T(8,128)(2,1)S(1)}, bf16[2,96,768]{2,1,0:T(8,128)(2,1)S(1)}, u32[]{:S(2)}, u32[]{:S(2)}) collective-permute-start(bf16[2,96,768]{2,1,0:T(8,128)(2,1)S(1)} %dynamic-slice_bitcast_fusion.3), channel_id=1, source_target_pairs={{0,8},{4,12},{8,0},{12,4},{16,24},{20,28},{24,16},{28,20},{1,9},{5... | collective-permute-start | bytes 884744 | tf_op jit(solution)/shard_map/ppermute | solution.py:325
  338.1 10.7 %collective-permute-start.14 = (bf16[2,96,768]{2,1,0:T(8,128)(2,1)S(1)}, bf16[2,96,768]{2,1,0:T(8,128)(2,1)S(1)}, u32[]{:S(2)}, u32[]{:S(2)}) collective-permute-start(bf16[2,96,768]{2,1,0:T(8,128)(2,1)S(1)} %dynamic-slice_bitcast_fusion.4), channel_id=1, source_target_pairs={{0,8},{4,12},{8,0},{12,4},{16,24},{20,28},{24,16},{28,20},{1,9},{5... | collective-permute-start | bytes 884744 | tf_op jit(solution)/shard_map/ppermute | solution.py:325
  339.9 11.0 %collective-permute-start.19 = (bf16[1,96,768]{2,1,0:T(8,128)(2,1)S(1)}, bf16[1,96,768]{2,1,0:T(8,128)(2,1)S(1)}, u32[]{:S(2)}, u32[]{:S(2)}) collective-permute-start(bf16[1,96,768]{2,1,0:T(8,128)(2,1)S(1)} %constant_dynamic-slice_fusion.2), channel_id=1, source_target_pairs={{0,16},{4,20},{8,24},{12,28},{16,0},{20,4},{24,8},{28,12},{1,17},{... | collective-permute-start | bytes 442376 | tf_op jit(solution)/shard_map/ppermute | solution.py:325
  348.9 8.4 %collective-permute-start.15 = (bf16[1,96,768]{2,1,0:T(8,128)(2,1)S(1)}, bf16[1,96,768]{2,1,0:T(8,128)(2,1)S(1)}, u32[]{:S(2)}, u32[]{:S(2)}) collective-permute-start(bf16[1,96,768]{2,1,0:T(8,128)(2,1)S(1)} %constant_dynamic-slice_fusion), channel_id=1, source_target_pairs={{0,16},{4,20},{8,24},{12,28},{16,0},{20,4},{24,8},{28,12},{1,17},{... | collective-permute-start | bytes 442376 | tf_op jit(solution)/shard_map/ppermute | solution.py:325
